TPU v7x, 512 devices: a whole 4x4x16 slice. The times are simulated.
512 devices in a mesh: dp: 32 (over z, core), tp: 16 (over y, x).
Axes of the slice: x: 4, y: 4, z: 16, core: 2. Of those that a mesh axis runs over, the one named last changes fastest.
Arguments:
- residual_rows: bfloat16 [4096, 7168], P(('dp', 'tp')), may hold values from -6 to 6
- norm_gain: float32 [7168], replicated, may hold values from 0.25 to 1.75
- gate_weight: bfloat16 [7168, 10240], P(None, 'tp'), may hold values from -0.0625 to 0.0625
- up_weight: bfloat16 [7168, 10240], P(None, 'tp'), may hold values from -0.0625 to 0.0625
- down_weight: bfloat16 [10240, 7168], P('tp', 'dp'), may hold values from -0.0625 to 0.0625
- row_count: int32 [512], P(('dp', 'tp')), may hold values from 1 to 8, as said below
Outputs:
- layer_out: bfloat16 [4096, 7168], P(('dp', 'tp'))
Inputs may be any that keep to these rules, and one draw needn't show every extreme that they name: `row_count`: every rank has at least one live row; some rank fills all 8 slots.
All inputs are finite; a program needn't handle non-finite values.
Results may differ from a plain program's by a relative error of at most 0.0046.
Values may be sent and summed in bfloat16 or wider, within the bound.
No kernel may reach another device: no remote copies, remote signals or barrier semaphores. Data moves between devices by JAX's collectives and lax.ppermute only.
A program may use at most 128 MiB of HBM per device.

v0:
```python
import jax
import jax.numpy as jnp
from jax import lax
from jax.sharding import PartitionSpec as P


def normalize(resid, norm_gain):
    scale = lax.rsqrt(jnp.mean(resid * resid, axis=1, keepdims=True) + 1e-06)
    return (resid * scale * norm_gain[None, :]).astype(jnp.bfloat16)


def shards(residual_rows, norm_gain, gate_weight, up_weight, down_weight, row_count):
    resid = residual_rows.astype(jnp.float32)
    gathered = lax.all_gather(normalize(resid, norm_gain), "tp", axis=0, tiled=True)
    gate = jnp.dot(gathered, gate_weight, preferred_element_type=jnp.float32)
    up = jnp.dot(gathered, up_weight, preferred_element_type=jnp.float32)
    hidden = (jax.nn.silu(gate) * up).astype(jnp.bfloat16)
    partial_terms = jnp.dot(
        hidden,
        lax.all_gather(down_weight, "dp", axis=1, tiled=True),
        preferred_element_type=jnp.float32,
    )
    own_rows = residual_rows.shape[0]
    ffn = lax.psum_scatter(partial_terms, "tp", scatter_dimension=0, tiled=True)
    slots = jnp.arange(own_rows, dtype=jnp.int32)
    live = (slots < row_count[0]).astype(jnp.float32)[:, None]
    return (live * (resid + ffn)).astype(jnp.bfloat16)


def solution(mesh):
    return jax.shard_map(
        shards,
        mesh=mesh,
        in_specs=(
            P(("dp", "tp"), None),
            P(),
            P(None, "tp"),
            P(None, "tp"),
            P("tp", "dp"),
            P(("dp", "tp")),
        ),
        out_specs=P(("dp", "tp"), None),
        check_vma=False,
    )
```

profile of v0, /device:TPU:1, one launch (start us, length us, event | category | flops | bytes accessed | tf_op | source)
XLA Modules:
  0.0 303.6 jit_solution(8451573839014913377)
XLA Ops:
  6.5 0.0 all-gather.3.cloned.1.call-start
  6.5 1.1 fusion.7
  7.6 1.6 fusion.9
  9.3 0.0 all-gather.3.cloned.1.call-update
  9.3 0.0 all-gather.5.cloned.1.call-start
  9.3 0.7 all-gather.5.cloned.1.call-update
  10.0 0.0 all-reduce.3.cloned.1.call-start
  10.1 64.1 %all-gather.3.cloned.1.call-done = bf16[128,7168]{1,0:T(8,128)(2,1)} async-done(((bf16[8,7168]{1,0:T(8,128)(2,1)}), bf16[128,7168]{1,0:T(8,128)(2,1)}) %all-gather.3.cloned.1.call-update) | async-done | bytes 1835024 | tf_op jit(solution)/shard_map/all_gather | solution.py:14
  74.2 0.0 copy-start
  74.2 5.9 %fusion.14 = f32[128,640]{1,0:T(8,128)S(1)} fusion(bf16[128,7168]{1,0:T(8,128)(2,1)} %all-gather.3.cloned.1.call-done, bf16[7168,640]{1,0:T(8,128)(2,1)} %param.8), kind=kOutput, calls=%fused_computation.20 | convolution fusion | flops 1174405120 | bytes 11337728 | tf_op jit(solution)/shard_map/dot_general | solution.py:15
  80.1 0.0 copy-start.1
  80.1 77.9 %all-gather.5.cloned.1.call-done = bf16[640,7168]{0,1:T(8,128)(2,1)} async-done(((bf16[640,224]{0,1:T(8,128)(2,1)}), bf16[640,7168]{0,1:T(8,128)(2,1)}) %all-gather.5.cloned.1.call-update) | async-done | bytes 9175056 | tf_op jit(solution)/shard_map/all_gather | solution.py:20
  158.0 0.0 copy-done
  158.0 12.5 %fusion.1 = f32[128,7168]{1,0:T(8,128)} fusion(bf16[640,7168]{0,1:T(8,128)(2,1)} %all-gather.5.cloned.1.call-done, bf16[128,7168]{1,0:T(8,128)(2,1)S(1)} %copy-done, bf16[7168,640]{1,0:T(8,128)(2,1)} %param.9, f32[128,640]{1,0:T(8,128)S(1)} %fusion.14), kind=kOutput, calls=%fused_computation.2 | convolution fusion | flops 2349301760 | bytes 24182784 | tf_op jit(solution)/shard_map/dot_general | solution.py:18
  170.5 0.0 all-reduce.3.cloned.1.call-update
  171.2 1.3 dynamic-slice
  173.1 122.3 %all-reduce.3.cloned.1.call-done = f32[128,7168]{1,0:T(8,128)} async-done(((f32[128,7168]{1,0:T(8,128)}), f32[128,7168]{1,0:T(8,128)}) %all-reduce.3.cloned.1.call-update) | async-done | bytes 3670032
  295.4 0.0 copy-done.1
  295.4 1.7 fusion.11
  (2 shorter events, 0.0 us)
Async XLA Ops:
  6.5 67.7 %all-gather.3.cloned.1.call-start = ((), (), s32[]{:S(2)}) async-start(), calls=%async_computation | async-start | bytes 1949696 | tf_op jit(solution)/shard_map/all_gather | solution.py:14
  9.3 148.7 %all-gather.5.cloned.1.call-start = ((), (), s32[]{:S(2)}) async-start(), calls=%async_computation.1 | async-start | bytes 9461760 | tf_op jit(solution)/shard_map/all_gather | solution.py:20
  10.0 285.3 %all-reduce.3.cloned.1.call-start = ((), (), s32[]{:S(2)}) async-start(), calls=%async_computation.2 | async-start | bytes 7340032
  74.2 83.8 %copy-start = (bf16[128,7168]{1,0:T(8,128)(2,1)S(1)}, bf16[128,7168]{1,0:T(8,128)(2,1)}, u32[]{:S(2)}) copy-start(bf16[128,7168]{1,0:T(8,128)(2,1)} %all-gather.3.cloned.1.call-done) | copy-start | bytes 5505028
  80.1 215.2 %copy-start.1 = (bf16[8,7168]{1,0:T(8,128)(2,1)S(1)}, bf16[8,7168]{1,0:T(8,128)(2,1)}, u32[]{:S(2)}) copy-start(bf16[8,7168]{1,0:T(8,128)(2,1)} %param.6) | copy-start | bytes 344068
Sparse Core Ops, SparseCore 0:
  10.4 63.8 all-gather.2
  76.4 81.6 all-gather.4
  170.6 124.6 all-reduce.2
where the time goes:
time: 304 us
  waiting for transfers between devices  265 us (87%)
  matrix products  18.4 us (6%)
  between operations  14.4 us (5%)
  other arithmetic  4.39 us (1%)
    unnamed x4, waiting for transfers between devices  123 us
    all_gather x1, waiting for transfers between devices, shards(): lax.all_gather(down_weight, 'dp', axis=1, tiled=True)  77.9 us
    all_gather x1, waiting for transfers between devices, shards(): lax.all_gather(normalize(resid, norm_gain), 'tp', axis=0, tiled=True)  64.1 us
    dot_general x1, matrix products, shards(): jnp.dot(hidden, lax.all_gather(down_weight, 'dp', axis=1, tiled=True), pr...  12.5 us
  transfers between devices with their start and end apart: 3, of which 3 were waited for; matrix products, arithmetic and copies ran while one was open for 2% of the time, Pallas kernels for 0%

commit v1 on v0

--- a/solution.py
+++ b/solution.py
@@ -10,18 +10,19 @@
 
 
 def shards(residual_rows, norm_gain, gate_weight, up_weight, down_weight, row_count):
+    own_rows, width = residual_rows.shape
+    ranks = lax.axis_size("tp")
     resid = residual_rows.astype(jnp.float32)
-    gathered = lax.all_gather(normalize(resid, norm_gain), "tp", axis=0, tiled=True)
+    down = lax.all_gather(down_weight, "dp", axis=1, tiled=True)
+    normed = jnp.broadcast_to(normalize(resid, norm_gain)[None], (ranks, own_rows, width))
+    gathered = lax.all_to_all(normed, "tp", 0, 0).reshape(ranks * own_rows, width)
     gate = jnp.dot(gathered, gate_weight, preferred_element_type=jnp.float32)
     up = jnp.dot(gathered, up_weight, preferred_element_type=jnp.float32)
     hidden = (jax.nn.silu(gate) * up).astype(jnp.bfloat16)
-    partial_terms = jnp.dot(
-        hidden,
-        lax.all_gather(down_weight, "dp", axis=1, tiled=True),
-        preferred_element_type=jnp.float32,
-    )
-    own_rows = residual_rows.shape[0]
-    ffn = lax.psum_scatter(partial_terms, "tp", scatter_dimension=0, tiled=True)
+    partial_terms = jnp.dot(hidden, down, preferred_element_type=jnp.float32)
+    partial_terms = partial_terms.astype(jnp.bfloat16).reshape(ranks, own_rows, width)
+    terms = lax.all_to_all(partial_terms, "tp", 0, 0)
+    ffn = jnp.sum(terms.astype(jnp.float32), axis=0)
     slots = jnp.arange(own_rows, dtype=jnp.int32)
     live = (slots < row_count[0]).astype(jnp.float32)[:, None]
     return (live * (resid + ffn)).astype(jnp.bfloat16)

time: 304 us -> 151 us (0.50)
  waiting for transfers between devices: 265 us -> 78.1 us
  blocking collectives: 0 us -> 31.2 us
  starting transfers between devices: 0.08 us -> 6.68 us
    unnamed x4 -> x1, waiting for transfers between devices: 123 us -> 0.71 us
    all_gather x2 -> x1, waiting for transfers between devices: 142 us -> 49.7 us  [shards(): down = lax.all_gather(down_weight, 'dp', axis=1, tiled=True)]
    all_to_all x0 -> x1, blocking collectives: none -> 31.2 us  [shards(): lax.all_to_all(normed, 'tp', 0, 0).reshape(ranks * own_rows, width)]
    all_to_all x0 -> x1, waiting for transfers between devices: none -> 27.7 us  [shards(): terms = lax.all_to_all(partial_terms, 'tp', 0, 0)]
    all_to_all x0 -> x1, starting transfers between devices: none -> 6.67 us  [shards(): terms = lax.all_to_all(partial_terms, 'tp', 0, 0)]
  transfers between devices with their start and end apart: 3 -> 2, of which waited for: 3 -> 2; matrix products, arithmetic and copies ran while one was open for 2% -> 5% of each run, Pallas kernels for 0% -> 0%
where the time goes in v1:
time: 151 us
  waiting for transfers between devices  78.1 us (52%)
  blocking collectives  31.2 us (21%)
  matrix products  17.3 us (11%)
  between operations  14.1 us (9%)
  starting transfers between devices  6.68 us (4%)
  other arithmetic  3.07 us (2%)
    all_gather x1, waiting for transfers between devices, shards(): down = lax.all_gather(down_weight, 'dp', axis=1, tiled=True)  49.7 us
    all_to_all x1, blocking collectives, shards(): lax.all_to_all(normed, 'tp', 0, 0).reshape(ranks * own_rows, width)  31.2 us
    all_to_all x1, waiting for transfers between devices, shards(): terms = lax.all_to_all(partial_terms, 'tp', 0, 0)  27.7 us
    dot_general x1, matrix products, shards(): partial_terms = jnp.dot(hidden, down, preferred_element_type=jnp.float32)  11.9 us
    all_to_all x1, starting transfers between devices, shards(): terms = lax.all_to_all(partial_terms, 'tp', 0, 0)  6.67 us
    dot_general x1, matrix products, shards(): gate = jnp.dot(gathered, gate_weight, preferred_element_type=jnp.float32)  5.39 us
  transfers between devices with their start and end apart: 2, of which 2 were waited for; matrix products, arithmetic and copies ran while one was open for 5% of the time, Pallas kernels for 0%

profile of v1, /device:TPU:1, one launch (start us, length us, event | category | flops | bytes accessed | tf_op | source)
XLA Modules:
  0.0 150.5 jit_solution(10016127695894025273)
XLA Ops:
  6.5 0.0 all-gather.2.cloned.1.call-start
  6.5 0.7 all-gather.2.cloned.1.call-update
  7.3 1.1 fusion.18
  8.3 1.0 fusion.20
  9.3 0.2 broadcast_in_dim.2
  9.5 31.2 %all_to_all.10 = bf16[16,8,7168]{2,1,0:T(8,128)(2,1)S(1)} all-to-all(bf16[16,8,7168]{2,1,0:T(8,128)(2,1)S(1)} %broadcast_in_dim.2), channel_id=1, replica_groups=mesh['dp'=32,'tp'=16] {'tp'}, dimensions={0} | all-to-all | bytes 3670016 | tf_op jit(solution)/shard_map/all_to_all | solution.py:18
  40.7 5.4 %fusion.3 = f32[128,640]{1,0:T(8,128)S(1)} fusion(bf16[7168,640]{1,0:T(8,128)(2,1)} %param.8, bf16[16,8,7168]{2,1,0:T(8,128)(2,1)S(1)} %all_to_all.10), kind=kOutput, calls=%fused_computation.5 | convolution fusion | flops 1174405120 | bytes 11337728 | tf_op jit(solution)/shard_map/dot_general | solution.py:19
  46.1 49.7 %all-gather.2.cloned.1.call-done = bf16[640,7168]{0,1:T(8,128)(2,1)} async-done(((bf16[640,224]{0,1:T(8,128)(2,1)}), bf16[640,7168]{0,1:T(8,128)(2,1)}) %all-gather.2.cloned.1.call-update) | async-done | bytes 9175056 | tf_op jit(solution)/shard_map/all_gather | solution.py:16
  95.7 11.9 %fusion = bf16[16,8,7168]{2,1,0:T(8,128)(2,1)} fusion(bf16[640,7168]{0,1:T(8,128)(2,1)} %all-gather.2.cloned.1.call-done, bf16[7168,640]{1,0:T(8,128)(2,1)} %param.9, bf16[16,8,7168]{2,1,0:T(8,128)(2,1)S(1)} %all_to_all.10, f32[128,640]{1,0:T(8,128)S(1)} %fusion.3), kind=kOutput, calls=%fused_computation.1 | convolution fusion | flops 2350219264 | bytes 22347776 | tf_op jit(solution)/shard_map/dot_general | solution.py:22
  107.7 0.0 copy-start
  107.7 6.7 %all-to-all-start.1 = ((bf16[16,8,7168]{2,1,0:T(8,128)(2,1)}), bf16[16,8,7168]{2,1,0:T(8,128)(2,1)S(1)}, u32[]{:S(2)}, u32[]{:S(2)}) async-start(bf16[16,8,7168]{2,1,0:T(8,128)(2,1)} %fusion), calls=%async_computation.1 | async-start | bytes 3670016 | tf_op jit(solution)/shard_map/all_to_all | solution.py:24
  115.0 27.7 %all-to-all-done.1 = bf16[16,8,7168]{2,1,0:T(8,128)(2,1)S(1)} async-done(((bf16[16,8,7168]{2,1,0:T(8,128)(2,1)}), bf16[16,8,7168]{2,1,0:T(8,128)(2,1)S(1)}, u32[]{:S(2)}, u32[]{:S(2)}) %all-to-all-start.1) | async-done | bytes 1835040 | tf_op jit(solution)/shard_map/all_to_all | solution.py:24
  142.7 0.3 convert_reduce_fusion
  142.9 0.0 copy-done
  143.0 0.7 fusion.22
  (2 shorter events, 0.0 us)
Async XLA Ops:
  6.5 89.2 %all-gather.2.cloned.1.call-start = ((), (), s32[]{:S(2)}) async-start(), calls=%async_computation.2 | async-start | bytes 9461760 | tf_op jit(solution)/shard_map/all_gather | solution.py:16
  107.7 35.3 %copy-start = (bf16[8,7168]{1,0:T(8,128)(2,1)S(1)}, bf16[8,7168]{1,0:T(8,128)(2,1)}, u32[]{:S(2)}) copy-start(bf16[8,7168]{1,0:T(8,128)(2,1)} %param.6) | copy-start | bytes 344068
  107.7 35.0 %all-to-all-start.1 = ((bf16[16,8,7168]{2,1,0:T(8,128)(2,1)}), bf16[16,8,7168]{2,1,0:T(8,128)(2,1)S(1)}, u32[]{:S(2)}, u32[]{:S(2)}) async-start(bf16[16,8,7168]{2,1,0:T(8,128)(2,1)} %fusion), calls=%async_computation.1 | async-start | bytes 3670016 | tf_op jit(solution)/shard_map/all_to_all | solution.py:24
Sparse Core Ops, SparseCore 0:
  9.5 86.2 all-gather.1

commit v2 on v1

--- a/solution.py
+++ b/solution.py
@@ -18,13 +18,14 @@
     gathered = lax.all_to_all(normed, "tp", 0, 0).reshape(ranks * own_rows, width)
     gate = jnp.dot(gathered, gate_weight, preferred_element_type=jnp.float32)
     up = jnp.dot(gathered, up_weight, preferred_element_type=jnp.float32)
-    hidden = (jax.nn.silu(gate) * up).astype(jnp.bfloat16)
+    hidden = lax.optimization_barrier((jax.nn.silu(gate) * up).astype(jnp.bfloat16))
     partial_terms = jnp.dot(hidden, down, preferred_element_type=jnp.float32)
     partial_terms = partial_terms.astype(jnp.bfloat16).reshape(ranks, own_rows, width)
+    slots = jnp.arange(own_rows, dtype=jnp.int32)
+    live = (slots < row_count[0]).astype(jnp.float32)[:, None]
+    partial_terms, resid, live = lax.optimization_barrier((partial_terms, resid, live))
     terms = lax.all_to_all(partial_terms, "tp", 0, 0)
     ffn = jnp.sum(terms.astype(jnp.float32), axis=0)
-    slots = jnp.arange(own_rows, dtype=jnp.int32)
-    live = (slots < row_count[0]).astype(jnp.float32)[:, None]
     return (live * (resid + ffn)).astype(jnp.bfloat16)
 
 

time: 151 us -> 142 us (0.940)
  waiting for transfers between devices: 78.1 us -> 66.4 us
    all_to_all x1, waiting for transfers between devices: 27.7 us -> 21.8 us  [shards(): lax.all_to_all(normed, 'tp', 0, 0).reshape(ranks * own_rows, width)]
    all_gather x1, waiting for transfers between devices: 49.7 us -> 44 us  [shards(): down = lax.all_gather(down_weight, 'dp', axis=1, tiled=True)]
    dot_general x0 -> x1, matrix products: none -> 5.41 us  [shards(): up = jnp.dot(gathered, up_weight, preferred_element_type=jnp.float32)]
    dot_general x1, matrix products: 11.9 us -> 6.57 us  [shards(): partial_terms = jnp.dot(hidden, down, preferred_element_type=jnp.float32)]
  transfers between devices with their start and end apart: 2 -> 2, of which waited for: 2 -> 2; matrix products, arithmetic and copies ran while one was open for 5% -> 10% of each run, Pallas kernels for 0% -> 0%
where the time goes in v2:
time: 142 us
  waiting for transfers between devices  66.4 us (47%)
  blocking collectives  31.7 us (22%)
  matrix products  17.4 us (12%)
  between operations  14.1 us (10%)
  starting transfers between devices  7.59 us (5%)
  other arithmetic  3.11 us (2%)
  local copies, waits for them, and re-layouts  1.44 us (1%)
    all_gather x1, waiting for transfers between devices, shards(): down = lax.all_gather(down_weight, 'dp', axis=1, tiled=True)  44 us
    all_to_all x1, blocking collectives, shards(): terms = lax.all_to_all(partial_terms, 'tp', 0, 0)  31.7 us
    all_to_all x1, waiting for transfers between devices, shards(): lax.all_to_all(normed, 'tp', 0, 0).reshape(ranks * own_rows, width)  21.8 us
    all_to_all x1, starting transfers between devices, shards(): lax.all_to_all(normed, 'tp', 0, 0).reshape(ranks * own_rows, width)  7.58 us
    dot_general x1, matrix products, shards(): partial_terms = jnp.dot(hidden, down, preferred_element_type=jnp.float32)  6.57 us
    dot_general x1, matrix products, shards(): up = jnp.dot(gathered, up_weight, preferred_element_type=jnp.float32)  5.41 us
    dot_general x1, matrix products, shards(): gate = jnp.dot(gathered, gate_weight, preferred_element_type=jnp.float32)  5.4 us
  transfers between devices with their start and end apart: 2, of which 2 were waited for; matrix products, arithmetic and copies ran while one was open for 10% of the time, Pallas kernels for 0%

profile of v2, /device:TPU:1, one launch (start us, length us, event | category | flops | bytes accessed | tf_op | source)
XLA Modules:
  0.0 141.7 jit_solution(9581354694338612356)
XLA Ops:
  6.5 0.0 copy-start
  6.5 0.0 all-gather.2.cloned.1.call-start
  6.5 0.7 all-gather.2.cloned.1.call-update
  7.3 1.1 multiply_reduce_fusion
  8.3 1.0 multiply_convert_fusion.1
  9.4 1.4 %broadcast_in_dim.2 = bf16[16,8,7168]{2,1,0:T(8,128)(2,1)} broadcast(bf16[8,7168]{1,0:T(8,128)(2,1)S(1)} %multiply_convert_fusion.1), dimensions={1,2} | broadcast | bytes 1949696 | tf_op jit(solution)/shard_map/broadcast_in_dim | solution.py:17
  10.8 7.6 %all-to-all-start = ((bf16[16,8,7168]{2,1,0:T(8,128)(2,1)}), bf16[16,8,7168]{2,1,0:T(8,128)(2,1)S(1)}, u32[]{:S(2)}, u32[]{:S(2)}) async-start(bf16[16,8,7168]{2,1,0:T(8,128)(2,1)} %broadcast_in_dim.2), calls=%async_computation | async-start | bytes 3670016 | tf_op jit(solution)/shard_map/all_to_all | solution.py:18
  18.4 0.0 copy-done
  19.1 21.8 %all-to-all-done = bf16[16,8,7168]{2,1,0:T(8,128)(2,1)S(1)} async-done(((bf16[16,8,7168]{2,1,0:T(8,128)(2,1)}), bf16[16,8,7168]{2,1,0:T(8,128)(2,1)S(1)}, u32[]{:S(2)}, u32[]{:S(2)}) %all-to-all-start) | async-done | bytes 1835040 | tf_op jit(solution)/shard_map/all_to_all | solution.py:18
  40.8 5.4 %fusion.3 = f32[128,640]{1,0:T(8,128)S(1)} fusion(bf16[7168,640]{1,0:T(8,128)(2,1)} %param.8, bf16[16,8,7168]{2,1,0:T(8,128)(2,1)S(1)} %all-to-all-done), kind=kOutput, calls=%fused_computation.5 | convolution fusion | flops 1174405120 | bytes 11337728 | tf_op jit(solution)/shard_map/dot_general | solution.py:19
  46.3 5.4 %fusion.8 = bf16[128,640]{1,0:T(8,128)(2,1)S(1)} fusion(bf16[7168,640]{1,0:T(8,128)(2,1)} %param.9, bf16[16,8,7168]{2,1,0:T(8,128)(2,1)S(1)} %all-to-all-done, f32[128,640]{1,0:T(8,128)S(1)} %fusion.3), kind=kOutput, calls=%fused_computation.8 | convolution fusion | flops 1174896640 | bytes 11501568 | tf_op jit(solution)/shard_map/dot_general | solution.py:20
  51.7 44.0 %all-gather.2.cloned.1.call-done = bf16[640,7168]{0,1:T(8,128)(2,1)} async-done(((bf16[640,224]{0,1:T(8,128)(2,1)}), bf16[640,7168]{0,1:T(8,128)(2,1)}) %all-gather.2.cloned.1.call-update) | async-done | bytes 9175056 | tf_op jit(solution)/shard_map/all_gather | solution.py:16
  95.6 6.6 %fusion = bf16[16,8,7168]{2,1,0:T(8,128)(2,1)S(1)} fusion(bf16[128,640]{1,0:T(8,128)(2,1)S(1)} %fusion.8, bf16[640,7168]{0,1:T(8,128)(2,1)} %all-gather.2.cloned.1.call-done), kind=kOutput, calls=%fused_computation.1 | convolution fusion | flops 1175322624 | bytes 11173888 | tf_op jit(solution)/shard_map/dot_general | solution.py:22
  102.2 31.7 %all_to_all.10 = bf16[16,8,7168]{2,1,0:T(8,128)(2,1)S(1)} all-to-all(bf16[16,8,7168]{2,1,0:T(8,128)(2,1)S(1)} %fusion), channel_id=1, replica_groups=mesh['dp'=32,'tp'=16] {'tp'}, dimensions={0} | all-to-all | bytes 3670016 | tf_op jit(solution)/shard_map/all_to_all | solution.py:27
  133.9 0.3 convert_reduce_fusion
  134.1 0.7 multiply_convert_fusion
  (3 shorter events, 0.0 us)
Async XLA Ops:
  6.5 11.9 %copy-start = (bf16[8,7168]{1,0:T(8,128)(2,1)S(1)}, bf16[8,7168]{1,0:T(8,128)(2,1)}, u32[]{:S(2)}) copy-start(bf16[8,7168]{1,0:T(8,128)(2,1)} %param.6) | copy-start | bytes 344068
  6.5 89.1 %all-gather.2.cloned.1.call-start = ((), (), s32[]{:S(2)}) async-start(), calls=%async_computation.2 | async-start | bytes 9461760 | tf_op jit(solution)/shard_map/all_gather | solution.py:16
  10.8 30.0 %all-to-all-start = ((bf16[16,8,7168]{2,1,0:T(8,128)(2,1)}), bf16[16,8,7168]{2,1,0:T(8,128)(2,1)S(1)}, u32[]{:S(2)}, u32[]{:S(2)}) async-start(bf16[16,8,7168]{2,1,0:T(8,128)(2,1)} %broadcast_in_dim.2), calls=%async_computation | async-start | bytes 3670016 | tf_op jit(solution)/shard_map/all_to_all | solution.py:18
Sparse Core Ops, SparseCore 0:
  9.5 86.1 all-gather.1

commit v3 on v2

v3 whole, which is shorter than its diff:
```python
import functools

import jax
import jax.numpy as jnp
from jax import lax
from jax.experimental import pallas as pl
from jax.experimental.pallas import tpu as pltpu
from jax.sharding import PartitionSpec as P

CORES = 2
NEAR = (-2, -1, 0, 1, 2)


def normalize(resid, norm_gain):
    scale = lax.rsqrt(jnp.mean(resid * resid, axis=1, keepdims=True) + 1e-06)
    return (resid * scale * norm_gain[None, :]).astype(jnp.bfloat16)


def dot_t(a, b):
    return lax.dot_general(a, b, (((1,), (1,)), ((), ())), preferred_element_type=jnp.float32)


def far_kernel(chips, first, count, hidden_ref, down_ref, out_ref, held, sems):
    features = held.shape[0] // count
    z = lax.axis_index("dp") // CORES
    copies = []
    for i in range(count):
        start = pl.multiple_of(lax.rem(z + (first + i), chips) * features, features)
        copy = pltpu.make_async_copy(
            down_ref.at[pl.ds(start, features), :],
            held.at[pl.ds(i * features, features), :],
            sems.at[i],
        )
        copy.start()
        copies.append(copy)
    for i in range(0, count, 2):
        stop = min(i + 2, count)
        for copy in copies[i:stop]:
            copy.wait()
        part = slice(i * features, stop * features)
        out_ref[:, part] = dot_t(hidden_ref[...], held[part, :]).astype(out_ref.dtype)


def far_terms(hidden, down, chips, first, count):
    rows, units = hidden.shape
    features = down.shape[0] // chips
    width = count * features
    return pl.pallas_call(
        functools.partial(far_kernel, chips, first, count),
        out_shape=jax.ShapeDtypeStruct((rows, width), jnp.bfloat16),
        in_specs=[pl.BlockSpec(memory_space=pltpu.VMEM), pl.BlockSpec(memory_space=pl.ANY)],
        out_specs=pl.BlockSpec(memory_space=pltpu.VMEM),
        scratch_shapes=[pltpu.VMEM((width, units), jnp.bfloat16), pltpu.SemaphoreType.DMA((count,))],
        compiler_params=pltpu.CompilerParams(vmem_limit_bytes=24 * 1024 * 1024),
        cost_estimate=pl.CostEstimate(
            flops=2 * rows * units * width, bytes_accessed=2 * width * (units + rows), transcendentals=0
        ),
        name="far_terms",
    )(hidden, down)


def summed(terms, ranks, own_rows):
    received = lax.all_to_all(terms.reshape(ranks, own_rows, -1), "tp", 0, 0)
    return jnp.sum(received.astype(jnp.float32), axis=0)


def shards(residual_rows, norm_gain, gate_weight, up_weight, down_weight, row_count):
    own_rows, width = residual_rows.shape
    ranks, groups = lax.axis_size("tp"), lax.axis_size("dp")
    chips = groups // CORES
    dp = lax.axis_index("dp")
    z, core = dp // CORES, dp % CORES
    resid = residual_rows.astype(jnp.float32)

    own = down_weight.T
    down = lax.all_gather(own, "dp", axis=0, tiled=True)

    def from_chip(step):
        if step == 0:
            return own
        return lax.ppermute(
            own, "dp", [((i + step * CORES) % groups, i) for i in range(groups)]
        )

    near = jnp.concatenate([from_chip(step) for step in NEAR], axis=0)
    near_other = lax.ppermute(near, "dp", [(i ^ 1, i) for i in range(groups)])

    normed = jnp.broadcast_to(normalize(resid, norm_gain)[None], (ranks, own_rows, width))
    gathered = lax.all_to_all(normed, "tp", 0, 0).reshape(ranks * own_rows, width)
    gate = jnp.dot(gathered, gate_weight, preferred_element_type=jnp.float32)
    up = jnp.dot(gathered, up_weight, preferred_element_type=jnp.float32)
    hidden = lax.optimization_barrier((jax.nn.silu(gate) * up).astype(jnp.bfloat16))

    near_terms = jnp.concatenate([dot_t(hidden, near), dot_t(hidden, near_other)], axis=1)
    near_sum = summed(near_terms.astype(jnp.bfloat16), ranks, own_rows)
    mine, other = jnp.split(near_sum.reshape(own_rows, CORES * len(NEAR), -1), 2, axis=1)
    first, second = jnp.where(core == 0, mine, other), jnp.where(core == 0, other, mine)
    near_sum = jnp.stack([first, second], axis=2).reshape(own_rows, -1)
    near_sum, hidden = lax.optimization_barrier((near_sum, hidden))

    far = far_terms(hidden, down, chips, NEAR[-1] + 1, chips - len(NEAR))
    slots = jnp.arange(own_rows, dtype=jnp.int32)
    live = (slots < row_count[0]).astype(jnp.float32)[:, None]
    far, resid, live = lax.optimization_barrier((far, resid, live))
    far_sum = summed(far, ranks, own_rows)
    ffn = jnp.roll(jnp.concatenate([near_sum, far_sum], axis=1), (z + NEAR[0]) * (width // chips), axis=1)
    return (live * (resid + ffn)).astype(jnp.bfloat16)


def solution(mesh):
    return jax.shard_map(
        shards,
        mesh=mesh,
        in_specs=(
            P(("dp", "tp"), None),
            P(),
            P(None, "tp"),
            P(None, "tp"),
            P("tp", "dp"),
            P(("dp", "tp")),
        ),
        out_specs=P(("dp", "tp"), None),
        check_vma=False,
    )
```

time: 142 us -> 155 us (1.092)
  starting transfers between devices: 7.59 us -> 44.4 us
  blocking collectives: 31.7 us -> 0 us
  local copies, waits for them, and re-layouts: 1.44 us -> 7.06 us
  Pallas kernels: 0 us -> 5.19 us
  matrix products: 17.4 us -> 13.2 us
    all_gather x1, waiting for transfers between devices: 44 us -> 8.51 us  [shards(): down = lax.all_gather(own, 'dp', axis=0, tiled=True)]
    all_to_all x1 -> x0, blocking collectives: 31.7 us -> none  [shards(): terms = lax.all_to_all(partial_terms, 'tp', 0, 0)]
    all_to_all x0 -> x2, waiting for transfers between devices: none -> 31.1 us  [summed(): received = lax.all_to_all(terms.reshape(ranks, own_rows, -1), 'tp', 0, 0)]
    ppermute x0 -> x5, waiting for transfers between devices: none -> 25.8 us  [the longest x4 25.8 us: from_chip(): lax.ppermute(own, 'dp', [((i + step * CORES) % groups, i) for i in range(...]
    ppermute x0 -> x5, starting transfers between devices: none -> 23.2 us  [the longest x4 19.2 us: from_chip(): lax.ppermute(own, 'dp', [((i + step * CORES) % groups, i) for i in range(...]
    all_to_all x1, waiting for transfers between devices: 21.8 us -> 0.01 us  [shards(): lax.all_to_all(normed, 'tp', 0, 0).reshape(ranks * own_rows, width)]
    all_to_all x0 -> x2, starting transfers between devices: none -> 13.6 us  [summed(): received = lax.all_to_all(terms.reshape(ranks, own_rows, -1), 'tp', 0, 0)]
    pallas_call x0 -> x1, Pallas kernels: none -> 5.19 us  [far_terms(): pl.pallas_call(functools.partial(far_kernel, chips, first, count), out_sh...]
  transfers between devices with their start and end apart: 2 -> 9, of which waited for: 2 -> 6; matrix products, arithmetic and copies ran while one was open for 10% -> 13% of each run, Pallas kernels for 0% -> 0%
where the time goes in v3:
time: 155 us; the launch traced here: 154 us
  waiting for transfers between devices  66.1 us (43%)
  starting transfers between devices  44.4 us (29%)
  between operations  14.3 us (9%)
  matrix products  13.2 us (9%)
  local copies, waits for them, and re-layouts  7.06 us (5%)
  Pallas kernels  5.19 us (3%)
  other arithmetic  4.17 us (3%)
    all_to_all x2, waiting for transfers between devices, summed(): received = lax.all_to_all(terms.reshape(ranks, own_rows, -1), 'tp', 0, 0)  31.1 us
    ppermute x4, waiting for transfers between devices, from_chip(): lax.ppermute(own, 'dp', [((i + step * CORES) % groups, i) for i in range(...  25.8 us
    ppermute x4, starting transfers between devices, from_chip(): lax.ppermute(own, 'dp', [((i + step * CORES) % groups, i) for i in range(...  19.2 us
    all_to_all x2, starting transfers between devices, summed(): received = lax.all_to_all(terms.reshape(ranks, own_rows, -1), 'tp', 0, 0)  13.6 us
    all_gather x1, waiting for transfers between devices, shards(): down = lax.all_gather(own, 'dp', axis=0, tiled=True)  8.51 us
    all_to_all x1, starting transfers between devices, shards(): lax.all_to_all(normed, 'tp', 0, 0).reshape(ranks * own_rows, width)  7.58 us
    dot_general x1, matrix products, shards(): up = jnp.dot(gathered, up_weight, preferred_element_type=jnp.float32)  5.39 us
    dot_general x1, matrix products, shards(): gate = jnp.dot(gathered, gate_weight, preferred_element_type=jnp.float32)  5.34 us
  transfers between devices with their start and end apart: 9, of which 6 were waited for; matrix products, arithmetic and copies ran while one was open for 13% of the time, Pallas kernels for 0%

profile of v3, /device:TPU:1, one launch (start us, length us, event | category | flops | bytes accessed | tf_op | source)
XLA Modules:
  0.0 154.4 jit_solution(7050129505813356172)
XLA Ops:
  7.3 1.1 multiply_reduce_fusion
  8.3 1.0 multiply_convert_fusion.1
  9.4 1.4 broadcast_in_dim.2
  10.8 7.6 %all-to-all-start = ((bf16[16,8,7168]{2,1,0:T(8,128)(2,1)}), bf16[16,8,7168]{2,1,0:T(8,128)(2,1)S(1)}, u32[]{:S(2)}, u32[]{:S(2)}) async-start(bf16[16,8,7168]{2,1,0:T(8,128)(2,1)} %broadcast_in_dim.2), calls=%async_computation | async-start | bytes 3670016 | tf_op jit(solution)/shard_map/all_to_all | solution.py:89
  18.4 4.9 %collective-permute-start = (bf16[224,640]{1,0:T(8,128)(2,1)}, bf16[224,640]{1,0:T(8,128)(2,1)S(1)}, u32[]{:S(2)}, u32[]{:S(2)}) collective-permute-start(bf16[224,640]{1,0:T(8,128)(2,1)} %bitcast.1), channel_id=1, source_target_pairs={{448,0},{464,16},{480,32},{496,48},{0,64},{16,80},{32,96},{48,112}... | collective-permute-start | bytes 860168 | tf_op jit(solution)/shard_map/ppermute | solution.py:81
  23.3 3.5 %collective-permute-start.1 = (bf16[224,640]{1,0:T(8,128)(2,1)}, bf16[224,640]{1,0:T(8,128)(2,1)S(1)}, u32[]{:S(2)}, u32[]{:S(2)}) collective-permute-start(bf16[224,640]{1,0:T(8,128)(2,1)} %bitcast.1), channel_id=1, source_target_pairs={{480,0},{496,16},{0,32},{16,48},{32,64},{48,80},{64,96},{80,112},{... | collective-permute-start | bytes 860168 | tf_op jit(solution)/shard_map/ppermute | solution.py:81
  26.8 6.5 %collective-permute-start.2 = (bf16[224,640]{1,0:T(8,128)(2,1)}, bf16[224,640]{1,0:T(8,128)(2,1)S(1)}, u32[]{:S(2)}, u32[]{:S(2)}) collective-permute-start(bf16[224,640]{1,0:T(8,128)(2,1)} %bitcast.1), channel_id=1, source_target_pairs={{32,0},{48,16},{64,32},{80,48},{96,64},{112,80},{128,96},{144,112}... | collective-permute-start | bytes 860168 | tf_op jit(solution)/shard_map/ppermute | solution.py:81
  33.4 4.3 %collective-permute-start.3 = (bf16[224,640]{1,0:T(8,128)(2,1)}, bf16[224,640]{1,0:T(8,128)(2,1)S(1)}, u32[]{:S(2)}, u32[]{:S(2)}) collective-permute-start(bf16[224,640]{1,0:T(8,128)(2,1)} %bitcast.1), channel_id=1, source_target_pairs={{64,0},{80,16},{96,32},{112,48},{128,64},{144,80},{160,96},{176,11... | collective-permute-start | bytes 860168 | tf_op jit(solution)/shard_map/ppermute | solution.py:81
  37.6 2.0 %collective-permute-done = bf16[224,640]{1,0:T(8,128)(2,1)S(1)} collective-permute-done((bf16[224,640]{1,0:T(8,128)(2,1)}, bf16[224,640]{1,0:T(8,128)(2,1)S(1)}, u32[]{:S(2)}, u32[]{:S(2)}) %collective-permute-start) | collective-permute-done | bytes 286752 | tf_op jit(solution)/shard_map/ppermute | solution.py:81
  39.7 19.1 %collective-permute-done.1 = bf16[224,640]{1,0:T(8,128)(2,1)S(1)} collective-permute-done((bf16[224,640]{1,0:T(8,128)(2,1)}, bf16[224,640]{1,0:T(8,128)(2,1)S(1)}, u32[]{:S(2)}, u32[]{:S(2)}) %collective-permute-start.1) | collective-permute-done | bytes 286752 | tf_op jit(solution)/shard_map/ppermute | solution.py:81
  58.8 1.0 constant_dynamic-update-slice_fusion.2
  59.8 4.7 %collective-permute-done.3 = bf16[224,640]{1,0:T(8,128)(2,1)S(1)} collective-permute-done((bf16[224,640]{1,0:T(8,128)(2,1)}, bf16[224,640]{1,0:T(8,128)(2,1)S(1)}, u32[]{:S(2)}, u32[]{:S(2)}) %collective-permute-start.3) | collective-permute-done | bytes 286752 | tf_op jit(solution)/shard_map/ppermute | solution.py:81
  64.5 4.0 %collective-permute-start.4 = (bf16[1120,640]{1,0:T(8,128)(2,1)S(1)}, bf16[1120,640]{1,0:T(8,128)(2,1)}, u32[]{:S(2)}, u32[]{:S(2)}) collective-permute-start(bf16[1120,640]{1,0:T(8,128)(2,1)S(1)} %constant_dynamic-update-slice_fusion), channel_id=1, source_target_pairs={{16,0},{0,16},{48,32},{32,48},{80,64},{64,80},{112,96},{96,112},{1... | collective-permute-start | bytes 4300808 | tf_op jit(solution)/shard_map/ppermute | solution.py:86
  68.6 5.3 %fusion.2 = f32[128,640]{1,0:T(8,128)S(1)} fusion(bf16[7168,640]{1,0:T(8,128)(2,1)} %param.8, bf16[16,8,7168]{2,1,0:T(8,128)(2,1)S(1)} %all-to-all-done), kind=kOutput, calls=%fused_computation.5 | convolution fusion | flops 1174405120 | bytes 11337728 | tf_op jit(solution)/shard_map/dot_general | solution.py:90
  73.9 5.4 %fusion.7.hidden_ref = bf16[128,640]{1,0:T(8,128)(2,1)S(1)} fusion(bf16[7168,640]{1,0:T(8,128)(2,1)} %param.9, bf16[16,8,7168]{2,1,0:T(8,128)(2,1)S(1)} %all-to-all-done, f32[128,640]{1,0:T(8,128)S(1)} %fusion.2), kind=kOutput, calls=%fused_computation.9 | convolution fusion | flops 1174896640 | bytes 11501568 | tf_op jit(solution)/shard_map/dot_general | solution.py:91
  79.3 1.9 %convolution_convert_fusion = bf16[128,1120]{0,1:T(8,128)(2,1)S(1)} fusion(bf16[128,640]{1,0:T(8,128)(2,1)S(1)} %fusion.7.hidden_ref, bf16[1120,640]{1,0:T(8,128)(2,1)} %collective-permute-done.4), kind=kOutput, calls=%fused_computation.1 | convolution fusion | flops 183644160 | bytes 1884160 | tf_op jit(solution)/shard_map/dot_general | solution.py:20
  82.2 1.0 pad_maximum_fusion
  83.2 6.8 %all-to-all-start.1 = ((bf16[16,8,2240]{2,1,0:T(8,128)(2,1)}), bf16[16,8,2240]{2,1,0:T(8,128)(2,1)S(1)}, u32[]{:S(2)}, u32[]{:S(2)}) async-start(bf16[16,8,2240]{2,1,0:T(8,128)(2,1)} %pad_maximum_fusion), calls=%async_computation.1 | async-start | bytes 1179648 | tf_op jit(solution)/shard_map/all_to_all | solution.py:63
  90.7 11.0 %all-to-all-done.1 = bf16[16,8,2240]{2,1,0:T(8,128)(2,1)S(1)} async-done(((bf16[16,8,2240]{2,1,0:T(8,128)(2,1)}), bf16[16,8,2240]{2,1,0:T(8,128)(2,1)S(1)}, u32[]{:S(2)}, u32[]{:S(2)}) %all-to-all-start.1) | async-done | bytes 573472 | tf_op jit(solution)/shard_map/all_to_all | solution.py:63
  102.2 8.5 %all-gather.2.cloned.1.call-done.down_ref = bf16[7168,640]{1,0:T(8,128)(2,1)} async-done(((bf16[224,640]{1,0:T(8,128)(2,1)}), bf16[7168,640]{1,0:T(8,128)(2,1)}) %all-gather.2.cloned.1.call-update) | async-done | bytes 9175056 | tf_op jit(solution)/shard_map/all_gather | solution.py:76
  110.7 3.6 %copy-done = bf16[7168,640]{1,0:T(8,128)(2,1)S(1)} copy-done((bf16[7168,640]{1,0:T(8,128)(2,1)S(1)}, bf16[7168,640]{1,0:T(8,128)(2,1)}, u32[]{:S(2)}) %copy-start) | copy-done | bytes 9175064
  114.3 5.2 %far_terms.1 = bf16[128,4928]{1,0:T(8,128)(2,1)} custom-call(bf16[128,640]{1,0:T(8,128)(2,1)S(1)} %fusion.7.hidden_ref, bf16[7168,640]{1,0:T(8,128)(2,1)S(1)} %copy-done), custom_call_target="tpu_custom_call" | custom-call | flops 807403520 | bytes 7569408 | tf_op jit(solution)/shard_map/far_terms/pallas_call | solution.py:48
  119.5 6.8 %all-to-all-start.2 = ((bf16[16,8,4928]{2,1,0:T(8,128)(2,1)}), bf16[16,8,4928]{2,1,0:T(8,128)(2,1)S(1)}, u32[]{:S(2)}, u32[]{:S(2)}) async-start(bf16[16,8,4928]{2,1,0:T(8,128)(2,1)} %bitcast.8), calls=%async_computation.2 | async-start | bytes 2555904 | tf_op jit(solution)/shard_map/all_to_all | solution.py:63
  126.3 20.1 %all-to-all-done.2 = bf16[16,8,4928]{2,1,0:T(8,128)(2,1)S(1)} async-done(((bf16[16,8,4928]{2,1,0:T(8,128)(2,1)}), bf16[16,8,4928]{2,1,0:T(8,128)(2,1)S(1)}, u32[]{:S(2)}, u32[]{:S(2)}) %all-to-all-start.2) | async-done | bytes 1261600 | tf_op jit(solution)/shard_map/all_to_all | solution.py:63
  (27 shorter events, 3.4 us)
Async XLA Ops:
  6.5 104.1 %all-gather.2.cloned.1.call-start = ((), (), s32[]{:S(2)}) async-start(), calls=%async_computation.3 | async-start | bytes 9461760 | tf_op jit(solution)/shard_map/all_gather | solution.py:76
  10.8 57.8 %all-to-all-start = ((bf16[16,8,7168]{2,1,0:T(8,128)(2,1)}), bf16[16,8,7168]{2,1,0:T(8,128)(2,1)S(1)}, u32[]{:S(2)}, u32[]{:S(2)}) async-start(bf16[16,8,7168]{2,1,0:T(8,128)(2,1)} %broadcast_in_dim.2), calls=%async_computation | async-start | bytes 3670016 | tf_op jit(solution)/shard_map/all_to_all | solution.py:89
  18.4 21.3 %collective-permute-start = (bf16[224,640]{1,0:T(8,128)(2,1)}, bf16[224,640]{1,0:T(8,128)(2,1)S(1)}, u32[]{:S(2)}, u32[]{:S(2)}) collective-permute-start(bf16[224,640]{1,0:T(8,128)(2,1)} %bitcast.1), channel_id=1, source_target_pairs={{448,0},{464,16},{480,32},{496,48},{0,64},{16,80},{32,96},{48,112}... | collective-permute-start | bytes 860168 | tf_op jit(solution)/shard_map/ppermute | solution.py:81
  23.3 35.5 %collective-permute-start.1 = (bf16[224,640]{1,0:T(8,128)(2,1)}, bf16[224,640]{1,0:T(8,128)(2,1)S(1)}, u32[]{:S(2)}, u32[]{:S(2)}) collective-permute-start(bf16[224,640]{1,0:T(8,128)(2,1)} %bitcast.1), channel_id=1, source_target_pairs={{480,0},{496,16},{0,32},{16,48},{32,64},{48,80},{64,96},{80,112},{... | collective-permute-start | bytes 860168 | tf_op jit(solution)/shard_map/ppermute | solution.py:81
  26.8 33.0 %collective-permute-start.2 = (bf16[224,640]{1,0:T(8,128)(2,1)}, bf16[224,640]{1,0:T(8,128)(2,1)S(1)}, u32[]{:S(2)}, u32[]{:S(2)}) collective-permute-start(bf16[224,640]{1,0:T(8,128)(2,1)} %bitcast.1), channel_id=1, source_target_pairs={{32,0},{48,16},{64,32},{80,48},{96,64},{112,80},{128,96},{144,112}... | collective-permute-start | bytes 860168 | tf_op jit(solution)/shard_map/ppermute | solution.py:81
  33.4 31.1 %collective-permute-start.3 = (bf16[224,640]{1,0:T(8,128)(2,1)}, bf16[224,640]{1,0:T(8,128)(2,1)S(1)}, u32[]{:S(2)}, u32[]{:S(2)}) collective-permute-start(bf16[224,640]{1,0:T(8,128)(2,1)} %bitcast.1), channel_id=1, source_target_pairs={{64,0},{80,16},{96,32},{112,48},{128,64},{144,80},{160,96},{176,11... | collective-permute-start | bytes 860168 | tf_op jit(solution)/shard_map/ppermute | solution.py:81
  64.5 14.8 %collective-permute-start.4 = (bf16[1120,640]{1,0:T(8,128)(2,1)S(1)}, bf16[1120,640]{1,0:T(8,128)(2,1)}, u32[]{:S(2)}, u32[]{:S(2)}) collective-permute-start(bf16[1120,640]{1,0:T(8,128)(2,1)S(1)} %constant_dynamic-update-slice_fusion), channel_id=1, source_target_pairs={{16,0},{0,16},{48,32},{32,48},{80,64},{64,80},{112,96},{96,112},{1... | collective-permute-start | bytes 4300808 | tf_op jit(solution)/shard_map/ppermute | solution.py:86
  82.0 8.0 %copy-start.1 = (bf16[8,7168]{1,0:T(8,128)(2,1)S(1)}, bf16[8,7168]{1,0:T(8,128)(2,1)}, u32[]{:S(2)}) copy-start(bf16[8,7168]{1,0:T(8,128)(2,1)} %param.6) | copy-start | bytes 344068
  83.2 18.5 %all-to-all-start.1 = ((bf16[16,8,2240]{2,1,0:T(8,128)(2,1)}), bf16[16,8,2240]{2,1,0:T(8,128)(2,1)S(1)}, u32[]{:S(2)}, u32[]{:S(2)}) async-start(bf16[16,8,2240]{2,1,0:T(8,128)(2,1)} %pad_maximum_fusion), calls=%async_computation.1 | async-start | bytes 1179648 | tf_op jit(solution)/shard_map/all_to_all | solution.py:63
  110.7 3.6 %copy-start = (bf16[7168,640]{1,0:T(8,128)(2,1)S(1)}, bf16[7168,640]{1,0:T(8,128)(2,1)}, u32[]{:S(2)}) copy-start(bf16[7168,640]{1,0:T(8,128)(2,1)} %all-gather.2.cloned.1.call-done.down_ref) | copy-start | bytes 27525124
  119.5 27.0 %all-to-all-start.2 = ((bf16[16,8,4928]{2,1,0:T(8,128)(2,1)}), bf16[16,8,4928]{2,1,0:T(8,128)(2,1)S(1)}, u32[]{:S(2)}, u32[]{:S(2)}) async-start(bf16[16,8,4928]{2,1,0:T(8,128)(2,1)} %bitcast.8), calls=%async_computation.2 | async-start | bytes 2555904 | tf_op jit(solution)/shard_map/all_to_all | solution.py:63
Sparse Core Ops, SparseCore 0:
  9.5 101.1 all-gather.1

commit v4 on v1

v4 whole, which is shorter than its diff:
```python
import functools

import jax
import jax.numpy as jnp
from jax import lax
from jax.experimental import pallas as pl
from jax.experimental.pallas import tpu as pltpu
from jax.sharding import PartitionSpec as P

LANES = 128
PADDED = 16
STEP = 2


def normalize(resid, norm_gain):
    scale = lax.rsqrt(jnp.mean(resid * resid, axis=1, keepdims=True) + 1e-06)
    return (resid * scale * norm_gain[None, :]).astype(jnp.bfloat16)


def down_kernel(hidden_ref, down_ref, out_ref):
    @pl.when(pl.program_id(0) == 0)
    def _():
        out_ref[...] = jnp.zeros_like(out_ref)

    total = out_ref[...]
    for i in range(STEP):
        block = down_ref[:, i].reshape(out_ref.shape[1], down_ref.shape[3])
        total += lax.dot_general(
            hidden_ref[i], block, (((1,), (1,)), ((), ())), preferred_element_type=jnp.float32
        )
    out_ref[...] = total


def down_projection(hidden, down):
    ranks, rows, units = hidden.shape
    groups = down.shape[0]
    features = groups * PADDED
    return pl.pallas_call(
        down_kernel,
        grid=(ranks // STEP,),
        out_shape=jax.ShapeDtypeStruct((rows, features), jnp.float32),
        in_specs=[
            pl.BlockSpec((STEP, rows, units), lambda i: (i, 0, 0)),
            pl.BlockSpec((groups, STEP, PADDED, units), lambda i: (0, i, 0, 0)),
        ],
        out_specs=pl.BlockSpec((rows, features), lambda i: (0, 0)),
        compiler_params=pltpu.CompilerParams(vmem_limit_bytes=56 * 1024 * 1024),
        cost_estimate=pl.CostEstimate(
            flops=2 * rows * ranks * units * features,
            bytes_accessed=2 * ranks * units * (features + rows),
            transcendentals=0,
        ),
        name="down_projection",
    )(hidden, down)


def order_kernel(groups, each, parts_ref, out_ref):
    ranks, rows = parts_ref.shape[:2]
    lane = lax.broadcasted_iota(jnp.int32, (rows, LANES), 1)
    tiles = {}

    def put(tile, start, stop, value):
        if tile not in tiles:
            tiles[tile] = value
        else:
            tiles[tile] = jnp.where((lane >= start) & (lane < stop), value, tiles[tile])

    done = 0
    for group in range(groups):
        source = group * PADDED
        for rank in range(ranks):
            target = (group * ranks + rank) * each
            tile, start = divmod(target, LANES)
            first = source // LANES * LANES
            value = parts_ref[rank, :, first : first + LANES]
            value = pltpu.roll(value, (start - source % LANES) % LANES, 1)
            put(tile, start, min(start + each, LANES), value)
            if start + each > LANES:
                put(tile + 1, 0, start + each - LANES, value)
            while done < tile or (done in tiles and (done + 1) * LANES <= target + each):
                out_ref[:, done * LANES : (done + 1) * LANES] = tiles.pop(done)
                done += 1


def in_order(parts, groups, each):
    ranks, rows, _ = parts.shape
    return pl.pallas_call(
        functools.partial(order_kernel, groups, each),
        out_shape=jax.ShapeDtypeStruct((rows, groups * ranks * each), jnp.float32),
        in_specs=[pl.BlockSpec(memory_space=pltpu.VMEM)],
        out_specs=pl.BlockSpec(memory_space=pltpu.VMEM),
        name="in_order",
    )(parts)


def to_all(x, ranks):
    return lax.all_to_all(jnp.broadcast_to(x[None], (ranks, *x.shape)), "tp", 0, 0)


def shards(residual_rows, norm_gain, gate_weight, up_weight, down_weight, row_count):
    own_rows, width = residual_rows.shape
    ranks, groups = lax.axis_size("tp"), lax.axis_size("dp")
    units, features = down_weight.shape
    each = features // ranks
    resid = residual_rows.astype(jnp.float32)

    split = jnp.pad(down_weight.T.reshape(ranks, each, units), ((0, 0), (0, PADDED - each), (0, 0)))
    mine = lax.all_to_all(split, "tp", 0, 0)
    down = lax.all_gather(mine, "dp", axis=0, tiled=False)

    normed, mine = lax.optimization_barrier((normalize(resid, norm_gain), mine))
    gathered = to_all(normed, ranks).reshape(ranks * own_rows, width)
    gate = jnp.dot(gathered, gate_weight, preferred_element_type=jnp.float32)
    up = jnp.dot(gathered, up_weight, preferred_element_type=jnp.float32)
    hidden = (jax.nn.silu(gate) * up).astype(jnp.bfloat16)
    hidden, resid = lax.optimization_barrier((to_all(hidden, ranks), resid))

    total = down_projection(hidden, down)
    total, resid = lax.optimization_barrier((total, resid))
    parts = lax.all_to_all(total.reshape(ranks, own_rows, -1), "tp", 0, 0)
    ffn = in_order(parts, groups, each)
    slots = jnp.arange(own_rows, dtype=jnp.int32)
    live = (slots < row_count[0]).astype(jnp.float32)[:, None]
    return (live * (resid + ffn)).astype(jnp.bfloat16)


def solution(mesh):
    return jax.shard_map(
        shards,
        mesh=mesh,
        in_specs=(
            P(("dp", "tp"), None),
            P(),
            P(None, "tp"),
            P(None, "tp"),
            P("tp", "dp"),
            P(("dp", "tp")),
        ),
        out_specs=P(("dp", "tp"), None),
        check_vma=False,
    )
```

time: 151 us -> 144 us (0.954)
  waiting for transfers between devices: 78.1 us -> 51.8 us
  Pallas kernels: 0 us -> 11.8 us
  matrix products: 17.3 us -> 7.24 us
  blocking collectives: 31.2 us -> 40.5 us
  starting transfers between devices: 6.68 us -> 10.5 us
  local copies, waits for them, and re-layouts: 0.17 us -> 3.82 us
    all_gather x1, waiting for transfers between devices: 49.7 us -> 14.2 us  [shards(): down = lax.all_gather(mine, 'dp', axis=0, tiled=False)]
    pallas_call x0 -> x2, Pallas kernels: none -> 11.8 us  [the longest x1 9.58 us: down_projection(): pl.pallas_call(down_kernel, grid=(ranks // STEP,), out_shape=jax.ShapeDty...]
    dot_general x1, matrix products: 11.9 us -> 1.65 us  [shards(): up = jnp.dot(gathered, up_weight, preferred_element_type=jnp.float32)]
    all_to_all x1 -> x2, waiting for transfers between devices: 27.7 us -> 37.6 us  [the longest x1 30.1 us: to_all(): lax.all_to_all(jnp.broadcast_to(x[None], (ranks, *x.shape)), 'tp', 0, 0)]
    all_to_all x1 -> x2, blocking collectives: 31.2 us -> 40.5 us  [the longest x1 25.1 us: to_all(): lax.all_to_all(jnp.broadcast_to(x[None], (ranks, *x.shape)), 'tp', 0, 0)]
    all_to_all x1 -> x2, starting transfers between devices: 6.67 us -> 10.5 us  [the longest x1 6.57 us: shards(): parts = lax.all_to_all(total.reshape(ranks, own_rows, -1), 'tp', 0, 0)]
    broadcast_in_dim x1 -> x2, local copies, waits for them, and re-layouts: 0.17 us -> 2.03 us  [to_all(): jnp.broadcast_to(x[None], (ranks, *x.shape))]
  transfers between devices with their start and end apart: 2 -> 3, of which waited for: 2 -> 3; matrix products, arithmetic and copies ran while one was open for 5% -> 8% of each run, Pallas kernels for 0% -> 0%
where the time goes in v4:
time: 144 us
  waiting for transfers between devices  51.8 us (36%)
  blocking collectives  40.5 us (28%)
  between operations  14.2 us (10%)
  Pallas kernels  11.8 us (8%)
  starting transfers between devices  10.5 us (7%)
  matrix products  7.24 us (5%)
  local copies, waits for them, and re-layouts  3.82 us (3%)
  other arithmetic  3.78 us (3%)
    all_to_all x1, waiting for transfers between devices, to_all(): lax.all_to_all(jnp.broadcast_to(x[None], (ranks, *x.shape)), 'tp', 0, 0)  30.1 us
    all_to_all x1, blocking collectives, to_all(): lax.all_to_all(jnp.broadcast_to(x[None], (ranks, *x.shape)), 'tp', 0, 0)  25.1 us
    all_to_all x1, blocking collectives, shards(): mine = lax.all_to_all(split, 'tp', 0, 0)  15.4 us
    all_gather x1, waiting for transfers between devices, shards(): down = lax.all_gather(mine, 'dp', axis=0, tiled=False)  14.2 us
    pallas_call x1, Pallas kernels, down_projection(): pl.pallas_call(down_kernel, grid=(ranks // STEP,), out_shape=jax.ShapeDty...  9.58 us
    all_to_all x1, waiting for transfers between devices, shards(): parts = lax.all_to_all(total.reshape(ranks, own_rows, -1), 'tp', 0, 0)  7.57 us
    all_to_all x1, starting transfers between devices, shards(): parts = lax.all_to_all(total.reshape(ranks, own_rows, -1), 'tp', 0, 0)  6.57 us
    dot_general x1, matrix products, shards(): gate = jnp.dot(gathered, gate_weight, preferred_element_type=jnp.float32)  5.59 us
  transfers between devices with their start and end apart: 3, of which 3 were waited for; matrix products, arithmetic and copies ran while one was open for 8% of the time, Pallas kernels for 0%

profile of v4, /device:TPU:1, one launch (start us, length us, event | category | flops | bytes accessed | tf_op | source)
XLA Modules:
  0.0 143.6 jit_solution(18120975756118586969)
XLA Ops:
  6.5 0.0 all-gather.3.cloned.1.call-start
  6.5 1.0 reshape.25
  7.6 15.4 %all_to_all.20 = bf16[16,16,640]{2,1,0:T(8,128)(2,1)} all-to-all(bf16[16,16,640]{2,1,0:T(8,128)(2,1)S(1)} %pad.4), channel_id=1, replica_groups=mesh['dp'=32,'tp'=16] {'tp'}, dimensions={0} | all-to-all | bytes 655360 | tf_op jit(solution)/shard_map/all_to_all | solution.py:108
  23.0 0.0 all-gather.3.cloned.1.call-update
  23.0 1.1 multiply_reduce_fusion
  24.1 1.0 multiply_convert_fusion.1
  25.1 0.2 broadcast_in_dim.4
  25.3 0.0 slice-start
  25.3 25.1 %all_to_all.21 = bf16[16,8,7168]{2,1,0:T(8,128)(2,1)S(1)} all-to-all(bf16[16,8,7168]{2,1,0:T(8,128)(2,1)S(1)} %broadcast_in_dim.4), channel_id=1, replica_groups=mesh['dp'=32,'tp'=16] {'tp'}, dimensions={0} | all-to-all | bytes 3670016 | tf_op jit(solution)/shard_map/all_to_all | solution.py:97
  50.5 5.6 %fusion.2 = f32[128,640]{1,0:T(8,128)S(1)} fusion(bf16[7168,640]{1,0:T(8,128)(2,1)} %param.8, bf16[16,8,7168]{2,1,0:T(8,128)(2,1)S(1)} %all_to_all.21), kind=kOutput, calls=%fused_computation.2 | convolution fusion | flops 1174405120 | bytes 11337728 | tf_op jit(solution)/shard_map/dot_general | solution.py:113
  56.1 0.0 slice-done
  56.1 0.0 slice-done.1
  56.1 1.7 %fusion.7 = bf16[128,640]{1,0:T(8,128)(2,1)S(1)} fusion(bf16[7168,640]{1,0:T(8,128)(2,1)S(1)} %bitcast.17, bf16[16,8,7168]{2,1,0:T(8,128)(2,1)S(1)} %all_to_all.21, f32[128,640]{1,0:T(8,128)S(1)} %fusion.2), kind=kOutput, calls=%fused_computation.5 | convolution fusion | flops 1174896640 | bytes 11501568 | tf_op jit(solution)/shard_map/dot_general | solution.py:114
  57.8 1.9 %broadcast_in_dim.5 = bf16[16,128,640]{2,1,0:T(8,128)(2,1)} broadcast(bf16[128,640]{1,0:T(8,128)(2,1)S(1)} %fusion.7), dimensions={1,2} | broadcast | bytes 2785280 | tf_op jit(solution)/shard_map/broadcast_in_dim | solution.py:97
  59.6 3.9 %all-to-all-start.2 = ((bf16[16,128,640]{2,1,0:T(8,128)(2,1)}), bf16[16,128,640]{2,1,0:T(8,128)(2,1)S(1)}, u32[]{:S(2)}, u32[]{:S(2)}) async-start(bf16[16,128,640]{2,1,0:T(8,128)(2,1)} %broadcast_in_dim.5), calls=%async_computation.2 | async-start | bytes 5242880 | tf_op jit(solution)/shard_map/all_to_all | solution.py:97
  63.5 0.0 copy-done.2
  63.6 30.1 %all-to-all-done.2.hidden_ref = bf16[16,128,640]{2,1,0:T(8,128)(2,1)S(1)} async-done(((bf16[16,128,640]{2,1,0:T(8,128)(2,1)}), bf16[16,128,640]{2,1,0:T(8,128)(2,1)S(1)}, u32[]{:S(2)}, u32[]{:S(2)}) %all-to-all-start.2) | async-done | bytes 2621472 | tf_op jit(solution)/shard_map/all_to_all | solution.py:97
  93.6 14.2 %all-gather.3.cloned.1.call-done = bf16[512,16,640]{2,1,0:T(8,128)(2,1)} async-done(((bf16[16,16,640]{2,1,0:T(8,128)(2,1)}), bf16[512,16,640]{2,1,0:T(8,128)(2,1)}) %all-gather.3.cloned.1.call-update) | async-done | bytes 10485776 | tf_op jit(solution)/shard_map/all_gather | solution.py:109
  107.8 9.6 %down_projection.1 = f32[128,512]{1,0:T(8,128)} custom-call(bf16[16,128,640]{2,1,0:T(8,128)(2,1)} %copy-done, bf16[32,16,16,640]{3,2,1,0:T(8,128)(2,1)} %bitcast.18), custom_call_target="tpu_custom_call" | custom-call | flops 1342177280 | bytes 13107200 | tf_op jit(solution)/shard_map/down_projection/pallas_call | solution.py:38
  117.4 6.6 %all-to-all-start.3 = ((f32[16,8,512]{2,1,0:T(8,128)}), f32[16,8,512]{2,1,0:T(8,128)S(1)}, u32[]{:S(2)}, u32[]{:S(2)}) async-start(f32[16,8,512]{2,1,0:T(8,128)} %bitcast.19), calls=%async_computation.3 | async-start | bytes 524288 | tf_op jit(solution)/shard_map/all_to_all | solution.py:120
  124.6 7.6 %all-to-all-done.3.parts_ref = f32[16,8,512]{2,1,0:T(8,128)S(1)} async-done(((f32[16,8,512]{2,1,0:T(8,128)}), f32[16,8,512]{2,1,0:T(8,128)S(1)}, u32[]{:S(2)}, u32[]{:S(2)}) %all-to-all-start.3) | async-done | bytes 262176 | tf_op jit(solution)/shard_map/all_to_all | solution.py:120
  132.2 0.7 copy-done.1
  132.9 2.2 %in_order.1 = f32[8,7168]{1,0:T(8,128)} custom-call(f32[16,8,512]{2,1,0:T(8,128)} %copy-done.1), custom_call_target="tpu_custom_call" | custom-call | tf_op jit(solution)/shard_map/in_order/pallas_call | solution.py:87
  135.1 1.7 %multiply_convert_fusion = bf16[8,7168]{1,0:T(8,128)(2,1)} fusion(f32[8,7168]{1,0:T(8,128)S(1)} %convert_element_type.22, f32[8,7168]{1,0:T(8,128)} %in_order.1, f32[8]{0:T(128)S(1)} %compare_convert_fusion), kind=kLoop, calls=%fused_computation.6 | loop fusion | flops 172032 | bytes 573472 | tf_op jit(solution)/shard_map/convert_element_type | solution.py:124
  (12 shorter events, 0.1 us)
Async XLA Ops:
  6.5 101.3 %all-gather.3.cloned.1.call-start = ((), (), s32[]{:S(2)}) async-start(), calls=%async_computation.4 | async-start | bytes 10813440 | tf_op jit(solution)/shard_map/all_gather | solution.py:109
  25.3 30.8 %slice-start = ((s8[9175040]{0:T(1024)(128)(4,1)}), s8[4194304]{0:T(1024)(128)(4,1)S(1)}, s32[]{:S(2)}) async-start(s8[9175040]{0:T(1024)(128)(4,1)} %bitcast.16), calls=%async_computation.5 | async-start | bytes 8388608
  50.5 5.6 %slice-start.1 = ((s8[9175040]{0:T(1024)(128)(4,1)}), s8[4194304]{0:T(1024)(128)(4,1)S(1)}, s32[]{:S(2)}) async-start(s8[9175040]{0:T(1024)(128)(4,1)} %bitcast.16), calls=%async_computation.6 | async-start | bytes 8388608
  50.5 5.6 %slice-start.2 = ((s8[9175040]{0:T(1024)(128)(4,1)}), s8[786432]{0:T(1024)(128)(4,1)S(1)}, s32[]{:S(2)}) async-start(s8[9175040]{0:T(1024)(128)(4,1)} %bitcast.16), calls=%async_computation.7 | async-start | bytes 1572864
  59.6 3.9 %copy-start.2 = (bf16[8,7168]{1,0:T(8,128)(2,1)S(1)}, bf16[8,7168]{1,0:T(8,128)(2,1)}, u32[]{:S(2)}) copy-start(bf16[8,7168]{1,0:T(8,128)(2,1)} %param.6) | copy-start | bytes 344068
  59.6 34.0 %all-to-all-start.2 = ((bf16[16,128,640]{2,1,0:T(8,128)(2,1)}), bf16[16,128,640]{2,1,0:T(8,128)(2,1)S(1)}, u32[]{:S(2)}, u32[]{:S(2)}) async-start(bf16[16,128,640]{2,1,0:T(8,128)(2,1)} %broadcast_in_dim.5), calls=%async_computation.2 | async-start | bytes 5242880 | tf_op jit(solution)/shard_map/all_to_all | solution.py:97
  93.6 14.2 %copy-start = (bf16[16,128,640]{2,1,0:T(8,128)(2,1)}, bf16[16,128,640]{2,1,0:T(8,128)(2,1)S(1)}, u32[]{:S(2)}) copy-start(bf16[16,128,640]{2,1,0:T(8,128)(2,1)S(1)} %all-to-all-done.2.hidden_ref) | copy-start | bytes 7864324
  117.4 14.8 %all-to-all-start.3 = ((f32[16,8,512]{2,1,0:T(8,128)}), f32[16,8,512]{2,1,0:T(8,128)S(1)}, u32[]{:S(2)}, u32[]{:S(2)}) async-start(f32[16,8,512]{2,1,0:T(8,128)} %bitcast.19), calls=%async_computation.3 | async-start | bytes 524288 | tf_op jit(solution)/shard_map/all_to_all | solution.py:120
  132.2 0.7 copy-start.1
Sparse Core Ops, SparseCore 0:
  23.2 84.5 all-gather.2

commit v5 on v4

--- a/solution.py
+++ b/solution.py
@@ -17,22 +17,29 @@
     return (resid * scale * norm_gain[None, :]).astype(jnp.bfloat16)
 
 
-def down_kernel(hidden_ref, down_ref, out_ref):
-    @pl.when(pl.program_id(0) == 0)
+def down_kernel(hidden_ref, down_ref, out_ref, total_ref):
+    step = pl.program_id(0)
+    features, rows = total_ref.shape
+    units = down_ref.shape[3]
+    block = jnp.concatenate([down_ref[:, i].reshape(features, units) for i in range(STEP)], axis=1)
+    hidden = hidden_ref[...].reshape(STEP * units, rows)
+    terms = jnp.dot(block, hidden, preferred_element_type=jnp.float32)
+
+    @pl.when(step == 0)
     def _():
-        out_ref[...] = jnp.zeros_like(out_ref)
+        total_ref[...] = terms
 
-    total = out_ref[...]
-    for i in range(STEP):
-        block = down_ref[:, i].reshape(out_ref.shape[1], down_ref.shape[3])
-        total += lax.dot_general(
-            hidden_ref[i], block, (((1,), (1,)), ((), ())), preferred_element_type=jnp.float32
-        )
-    out_ref[...] = total
+    @pl.when(step > 0)
+    def _():
+        total_ref[...] += terms
+
+    @pl.when(step == pl.num_programs(0) - 1)
+    def _():
+        out_ref[...] = total_ref[...].T
 
 
 def down_projection(hidden, down):
-    ranks, rows, units = hidden.shape
+    ranks, units, rows = hidden.shape
     groups = down.shape[0]
     features = groups * PADDED
     return pl.pallas_call(
@@ -40,10 +47,11 @@
         grid=(ranks // STEP,),
         out_shape=jax.ShapeDtypeStruct((rows, features), jnp.float32),
         in_specs=[
-            pl.BlockSpec((STEP, rows, units), lambda i: (i, 0, 0)),
+            pl.BlockSpec((STEP, units, rows), lambda i: (i, 0, 0)),
             pl.BlockSpec((groups, STEP, PADDED, units), lambda i: (0, i, 0, 0)),
         ],
         out_specs=pl.BlockSpec((rows, features), lambda i: (0, 0)),
+        scratch_shapes=[pltpu.VMEM((features, rows), jnp.float32)],
         compiler_params=pltpu.CompilerParams(vmem_limit_bytes=56 * 1024 * 1024),
         cost_estimate=pl.CostEstimate(
             flops=2 * rows * ranks * units * features,
@@ -54,8 +62,10 @@
     )(hidden, down)
 
 
-def order_kernel(groups, each, parts_ref, out_ref):
+def finish_kernel(groups, each, count_ref, parts_ref, resid_ref, out_ref):
     ranks, rows = parts_ref.shape[:2]
+    slots = lax.broadcasted_iota(jnp.int32, (rows, LANES), 0)
+    live = (slots < count_ref[0]).astype(jnp.float32)
     lane = lax.broadcasted_iota(jnp.int32, (rows, LANES), 1)
     tiles = {}
 
@@ -78,19 +88,24 @@
             if start + each > LANES:
                 put(tile + 1, 0, start + each - LANES, value)
             while done < tile or (done in tiles and (done + 1) * LANES <= target + each):
-                out_ref[:, done * LANES : (done + 1) * LANES] = tiles.pop(done)
+                part = slice(done * LANES, (done + 1) * LANES)
+                resid = resid_ref[:, part].astype(jnp.float32)
+                out_ref[:, part] = (live * (resid + tiles.pop(done))).astype(out_ref.dtype)
                 done += 1
 
 
-def in_order(parts, groups, each):
-    ranks, rows, _ = parts.shape
+def finish(row_count, parts, residual_rows, groups, each):
     return pl.pallas_call(
-        functools.partial(order_kernel, groups, each),
-        out_shape=jax.ShapeDtypeStruct((rows, groups * ranks * each), jnp.float32),
-        in_specs=[pl.BlockSpec(memory_space=pltpu.VMEM)],
+        functools.partial(finish_kernel, groups, each),
+        out_shape=jax.ShapeDtypeStruct(residual_rows.shape, residual_rows.dtype),
+        in_specs=[
+            pl.BlockSpec(memory_space=pltpu.SMEM),
+            pl.BlockSpec(memory_space=pltpu.VMEM),
+            pl.BlockSpec(memory_space=pltpu.VMEM),
+        ],
         out_specs=pl.BlockSpec(memory_space=pltpu.VMEM),
-        name="in_order",
-    )(parts)
+        name="finish",
+    )(row_count, parts, residual_rows)
 
 
 def to_all(x, ranks):
@@ -113,15 +128,12 @@
     gate = jnp.dot(gathered, gate_weight, preferred_element_type=jnp.float32)
     up = jnp.dot(gathered, up_weight, preferred_element_type=jnp.float32)
     hidden = (jax.nn.silu(gate) * up).astype(jnp.bfloat16)
-    hidden, resid = lax.optimization_barrier((to_all(hidden, ranks), resid))
+    hidden = to_all(hidden.T, ranks)
 
     total = down_projection(hidden, down)
-    total, resid = lax.optimization_barrier((total, resid))
+    total, residual_rows, row_count = lax.optimization_barrier((total, residual_rows, row_count))
     parts = lax.all_to_all(total.reshape(ranks, own_rows, -1), "tp", 0, 0)
-    ffn = in_order(parts, groups, each)
-    slots = jnp.arange(own_rows, dtype=jnp.int32)
-    live = (slots < row_count[0]).astype(jnp.float32)[:, None]
-    return (live * (resid + ffn)).astype(jnp.bfloat16)
+    return finish(row_count, parts, residual_rows, groups, each)
 
 
 def solution(mesh):

time: 144 us -> 143 us (level)
  blocking collectives: 40.5 us -> 74.1 us
  waiting for transfers between devices: 51.8 us -> 23.4 us
  starting transfers between devices: 10.5 us -> 6.6 us
  other arithmetic: 3.78 us -> 2.08 us
    all_to_all x1 -> x2, blocking collectives: 25.1 us -> 58.7 us  [to_all(): lax.all_to_all(jnp.broadcast_to(x[None], (ranks, *x.shape)), 'tp', 0, 0)]
    all_to_all x1 -> x0, waiting for transfers between devices: 30.1 us -> none  [to_all(): lax.all_to_all(jnp.broadcast_to(x[None], (ranks, *x.shape)), 'tp', 0, 0)]
    all_to_all x1 -> x0, starting transfers between devices: 3.89 us -> none  [to_all(): lax.all_to_all(jnp.broadcast_to(x[None], (ranks, *x.shape)), 'tp', 0, 0)]
    convert_element_type x3 -> x0, other arithmetic: 1.69 us -> none  [the longest x1 1.66 us: shards(): return (live * (resid + ffn)).astype(jnp.bfloat16)]
    all_gather x1, waiting for transfers between devices: 14.2 us -> 15.8 us  [shards(): down = lax.all_gather(mine, 'dp', axis=0, tiled=False)]
  transfers between devices with their start and end apart: 3 -> 2, of which waited for: 3 -> 2; matrix products, arithmetic and copies ran while one was open for 8% -> 7% of each run, Pallas kernels for 0% -> 0%
where the time goes in v5:
time: 143 us; the launch traced here: 142 us
  blocking collectives  74.1 us (52%)
  waiting for transfers between devices  23.4 us (16%)
  between operations  14.1 us (10%)
  Pallas kernels  11.8 us (8%)
  matrix products  7.24 us (5%)
  starting transfers between devices  6.6 us (5%)
  local copies, waits for them, and re-layouts  2.63 us (2%)
  other arithmetic  2.08 us (1%)
    all_to_all x2, blocking collectives, to_all(): lax.all_to_all(jnp.broadcast_to(x[None], (ranks, *x.shape)), 'tp', 0, 0)  58.7 us
    all_gather x1, waiting for transfers between devices, shards(): down = lax.all_gather(mine, 'dp', axis=0, tiled=False)  15.8 us
    all_to_all x1, blocking collectives, shards(): mine = lax.all_to_all(split, 'tp', 0, 0)  15.4 us
    pallas_call x1, Pallas kernels, down_projection(): pl.pallas_call(down_kernel, grid=(ranks // STEP,), out_shape=jax.ShapeDty...  9.6 us
    all_to_all x1, waiting for transfers between devices, shards(): parts = lax.all_to_all(total.reshape(ranks, own_rows, -1), 'tp', 0, 0)  7.59 us
    all_to_all x1, starting transfers between devices, shards(): parts = lax.all_to_all(total.reshape(ranks, own_rows, -1), 'tp', 0, 0)  6.6 us
    dot_general x1, matrix products, shards(): gate = jnp.dot(gathered, gate_weight, preferred_element_type=jnp.float32)  5.59 us
  transfers between devices with their start and end apart: 2, of which 2 were waited for; matrix products, arithmetic and copies ran while one was open for 7% of the time, Pallas kernels for 0%

profile of v5, /device:TPU:1, one launch (start us, length us, event | category | flops | bytes accessed | tf_op | source)
XLA Modules:
  0.0 142.1 jit_solution(648591310445658149)
XLA Ops:
  6.5 0.0 all-gather.3.cloned.1.call-start
  6.5 1.0 reshape.20
  7.6 15.4 %all_to_all.20 = bf16[16,16,640]{2,1,0:T(8,128)(2,1)} all-to-all(bf16[16,16,640]{2,1,0:T(8,128)(2,1)S(1)} %pad.4), channel_id=1, replica_groups=mesh['dp'=32,'tp'=16] {'tp'}, dimensions={0} | all-to-all | bytes 655360 | tf_op jit(solution)/shard_map/all_to_all | solution.py:123
  23.0 0.0 all-gather.3.cloned.1.call-update
  23.0 1.1 fusion.16
  24.1 1.0 fusion.18
  25.1 0.2 broadcast_in_dim.4
  25.3 0.0 slice-start
  25.3 25.1 %all_to_all.21 = bf16[16,8,7168]{2,1,0:T(8,128)(2,1)S(1)} all-to-all(bf16[16,8,7168]{2,1,0:T(8,128)(2,1)S(1)} %broadcast_in_dim.4), channel_id=1, replica_groups=mesh['dp'=32,'tp'=16] {'tp'}, dimensions={0} | all-to-all | bytes 3670016 | tf_op jit(solution)/shard_map/all_to_all | solution.py:112
  50.5 0.0 slice-start.1
  50.5 5.6 %fusion.4 = f32[640,128]{0,1:T(8,128)S(1)} fusion(bf16[7168,640]{1,0:T(8,128)(2,1)} %param.8, bf16[16,8,7168]{2,1,0:T(8,128)(2,1)S(1)} %all_to_all.21), kind=kOutput, calls=%fused_computation.4 | convolution fusion | flops 1174405120 | bytes 11337728 | tf_op jit(solution)/shard_map/dot_general | solution.py:128
  56.0 0.0 slice-done
  56.1 0.0 slice-done.1
  56.1 0.0 slice-done.2
  56.1 1.7 %fusion.13 = bf16[640,128]{0,1:T(8,128)(2,1)S(1)} fusion(bf16[7168,640]{1,0:T(8,128)(2,1)S(1)} %bitcast.27, bf16[16,8,7168]{2,1,0:T(8,128)(2,1)S(1)} %all_to_all.21, f32[640,128]{0,1:T(8,128)S(1)} %fusion.4), kind=kOutput, calls=%fused_computation.7 | convolution fusion | flops 1174896640 | bytes 11501568 | tf_op jit(solution)/shard_map/dot_general | solution.py:129
  57.7 0.2 copy.9
  57.9 0.5 broadcast_in_dim.5
  58.4 33.6 %all_to_all.22.hidden_ref = bf16[16,640,128]{2,1,0:T(8,128)(2,1)} all-to-all(bf16[16,640,128]{2,1,0:T(8,128)(2,1)S(1)} %broadcast_in_dim.5), channel_id=1, replica_groups=mesh['dp'=32,'tp'=16] {'tp'}, dimensions={0} | all-to-all | bytes 5242880 | tf_op jit(solution)/shard_map/all_to_all | solution.py:112
  92.0 15.8 %all-gather.3.cloned.1.call-done = bf16[512,16,640]{2,1,0:T(8,128)(2,1)} async-done(((bf16[16,16,640]{2,1,0:T(8,128)(2,1)}), bf16[512,16,640]{2,1,0:T(8,128)(2,1)}) %all-gather.3.cloned.1.call-update) | async-done | bytes 10485776 | tf_op jit(solution)/shard_map/all_gather | solution.py:124
  107.9 9.6 %down_projection.1 = f32[128,512]{1,0:T(8,128)} custom-call(bf16[16,640,128]{2,1,0:T(8,128)(2,1)} %all_to_all.22.hidden_ref, bf16[32,16,16,640]{3,2,1,0:T(8,128)(2,1)} %bitcast.28), custom_call_target="tpu_custom_call" | custom-call | flops 1342177280 | bytes 13107200 | tf_op jit(solution)/shard_map/down_projection/pallas_call | solution.py:45
  117.5 6.6 %all-to-all-start.3 = ((f32[16,8,512]{2,1,0:T(8,128)}), f32[16,8,512]{2,1,0:T(8,128)S(1)}, u32[]{:S(2)}, u32[]{:S(2)}) async-start(f32[16,8,512]{2,1,0:T(8,128)} %bitcast.29), calls=%async_computation.3 | async-start | bytes 524288 | tf_op jit(solution)/shard_map/all_to_all | solution.py:135
  124.7 7.6 %all-to-all-done.3.parts_ref = f32[16,8,512]{2,1,0:T(8,128)S(1)} async-done(((f32[16,8,512]{2,1,0:T(8,128)}), f32[16,8,512]{2,1,0:T(8,128)S(1)}, u32[]{:S(2)}, u32[]{:S(2)}) %all-to-all-start.3) | async-done | bytes 262176 | tf_op jit(solution)/shard_map/all_to_all | solution.py:135
  132.3 0.7 copy-done
  133.0 2.2 %finish.1 = bf16[8,7168]{1,0:T(8,128)(2,1)} custom-call(s32[1]{0:T(128)S(6)} %copy.10.count_ref, f32[16,8,512]{2,1,0:T(8,128)} %copy-done, bf16[8,7168]{1,0:T(8,128)(2,1)} %resid_ref), custom_call_target="tpu_custom_call" | custom-call | tf_op jit(solution)/shard_map/finish/pallas_call | solution.py:98
  (5 shorter events, 0.0 us)
Async XLA Ops:
  6.5 101.3 %all-gather.3.cloned.1.call-start = ((), (), s32[]{:S(2)}) async-start(), calls=%async_computation.4 | async-start | bytes 10813440 | tf_op jit(solution)/shard_map/all_gather | solution.py:124
  25.3 30.8 %slice-start = ((s8[9175040]{0:T(1024)(128)(4,1)}), s8[4194304]{0:T(1024)(128)(4,1)S(1)}, s32[]{:S(2)}) async-start(s8[9175040]{0:T(1024)(128)(4,1)} %bitcast.26), calls=%async_computation.5 | async-start | bytes 8388608
  50.5 5.6 %slice-start.1 = ((s8[9175040]{0:T(1024)(128)(4,1)}), s8[4194304]{0:T(1024)(128)(4,1)S(1)}, s32[]{:S(2)}) async-start(s8[9175040]{0:T(1024)(128)(4,1)} %bitcast.26), calls=%async_computation.6 | async-start | bytes 8388608
  50.5 5.6 %slice-start.2 = ((s8[9175040]{0:T(1024)(128)(4,1)}), s8[786432]{0:T(1024)(128)(4,1)S(1)}, s32[]{:S(2)}) async-start(s8[9175040]{0:T(1024)(128)(4,1)} %bitcast.26), calls=%async_computation.7 | async-start | bytes 1572864
  117.5 14.8 %all-to-all-start.3 = ((f32[16,8,512]{2,1,0:T(8,128)}), f32[16,8,512]{2,1,0:T(8,128)S(1)}, u32[]{:S(2)}, u32[]{:S(2)}) async-start(f32[16,8,512]{2,1,0:T(8,128)} %bitcast.29), calls=%async_computation.3 | async-start | bytes 524288 | tf_op jit(solution)/shard_map/all_to_all | solution.py:135
  132.3 0.7 copy-start
Sparse Core Ops, SparseCore 0:
  23.2 84.6 all-gather.2

commit v6 on v5

--- a/solution.py
+++ b/solution.py
@@ -9,7 +9,8 @@
 
 LANES = 128
 PADDED = 16
-STEP = 2
+CHUNK = 8
+VMEM_LIMIT = 56 * 1024 * 1024
 
 
 def normalize(resid, norm_gain):
@@ -17,25 +18,26 @@
     return (resid * scale * norm_gain[None, :]).astype(jnp.bfloat16)
 
 
-def down_kernel(hidden_ref, down_ref, out_ref, total_ref):
-    step = pl.program_id(0)
-    features, rows = total_ref.shape
-    units = down_ref.shape[3]
-    block = jnp.concatenate([down_ref[:, i].reshape(features, units) for i in range(STEP)], axis=1)
-    hidden = hidden_ref[...].reshape(STEP * units, rows)
-    terms = jnp.dot(block, hidden, preferred_element_type=jnp.float32)
-
-    @pl.when(step == 0)
-    def _():
-        total_ref[...] = terms
-
-    @pl.when(step > 0)
-    def _():
-        total_ref[...] += terms
-
-    @pl.when(step == pl.num_programs(0) - 1)
-    def _():
-        out_ref[...] = total_ref[...].T
+def down_kernel(hidden_ref, down_ref, out_ref, held, sems):
+    groups, ranks, padded, units = held.shape
+    copies = []
+    for i in range(groups // CHUNK):
+        part = pl.ds(i * CHUNK, CHUNK)
+        copy = pltpu.make_async_copy(down_ref.at[part], held.at[part], sems.at[i])
+        copy.start()
+        copies.append(copy)
+    features = CHUNK * padded
+    for i, copy in enumerate(copies):
+        copy.wait()
+        total = None
+        for j in range(0, ranks, 2):
+            block = jnp.concatenate(
+                [held[i * CHUNK : (i + 1) * CHUNK, k].reshape(features, units) for k in (j, j + 1)], axis=1
+            )
+            hidden = hidden_ref[j : j + 2].reshape(2 * units, -1)
+            terms = jnp.dot(block, hidden, preferred_element_type=jnp.float32)
+            total = terms if total is None else total + terms
+        out_ref[:, i * features : (i + 1) * features] = total.T
 
 
 def down_projection(hidden, down):
@@ -44,15 +46,14 @@
     features = groups * PADDED
     return pl.pallas_call(
         down_kernel,
-        grid=(ranks // STEP,),
         out_shape=jax.ShapeDtypeStruct((rows, features), jnp.float32),
-        in_specs=[
-            pl.BlockSpec((STEP, units, rows), lambda i: (i, 0, 0)),
-            pl.BlockSpec((groups, STEP, PADDED, units), lambda i: (0, i, 0, 0)),
+        in_specs=[pl.BlockSpec(memory_space=pltpu.VMEM), pl.BlockSpec(memory_space=pl.ANY)],
+        out_specs=pl.BlockSpec(memory_space=pltpu.VMEM),
+        scratch_shapes=[
+            pltpu.VMEM(down.shape, jnp.bfloat16),
+            pltpu.SemaphoreType.DMA((groups // CHUNK,)),
         ],
-        out_specs=pl.BlockSpec((rows, features), lambda i: (0, 0)),
-        scratch_shapes=[pltpu.VMEM((features, rows), jnp.float32)],
-        compiler_params=pltpu.CompilerParams(vmem_limit_bytes=56 * 1024 * 1024),
+        compiler_params=pltpu.CompilerParams(vmem_limit_bytes=VMEM_LIMIT),
         cost_estimate=pl.CostEstimate(
             flops=2 * rows * ranks * units * features,
             bytes_accessed=2 * ranks * units * (features + rows),
@@ -62,7 +63,9 @@
     )(hidden, down)
 
 
-def finish_kernel(groups, each, count_ref, parts_ref, resid_ref, out_ref):
+def finish_kernel(groups, each, count_ref, parts_ref, resid_ref, out_ref, resid, ffn, sem):
+    copy = pltpu.make_async_copy(resid_ref, resid, sem)
+    copy.start()
     ranks, rows = parts_ref.shape[:2]
     slots = lax.broadcasted_iota(jnp.int32, (rows, LANES), 0)
     live = (slots < count_ref[0]).astype(jnp.float32)
@@ -88,24 +91,32 @@
             if start + each > LANES:
                 put(tile + 1, 0, start + each - LANES, value)
             while done < tile or (done in tiles and (done + 1) * LANES <= target + each):
-                part = slice(done * LANES, (done + 1) * LANES)
-                resid = resid_ref[:, part].astype(jnp.float32)
-                out_ref[:, part] = (live * (resid + tiles.pop(done))).astype(out_ref.dtype)
+                ffn[:, done * LANES : (done + 1) * LANES] = tiles.pop(done)
                 done += 1
+    copy.wait()
+    for i in range(done):
+        part = slice(i * LANES, (i + 1) * LANES)
+        out_ref[:, part] = (live * (resid[:, part] + ffn[:, part])).astype(out_ref.dtype)
 
 
-def finish(row_count, parts, residual_rows, groups, each):
+def finish(row_count, parts, resid, groups, each):
     return pl.pallas_call(
         functools.partial(finish_kernel, groups, each),
-        out_shape=jax.ShapeDtypeStruct(residual_rows.shape, residual_rows.dtype),
+        out_shape=jax.ShapeDtypeStruct(resid.shape, jnp.bfloat16),
         in_specs=[
             pl.BlockSpec(memory_space=pltpu.SMEM),
             pl.BlockSpec(memory_space=pltpu.VMEM),
-            pl.BlockSpec(memory_space=pltpu.VMEM),
+            pl.BlockSpec(memory_space=pl.ANY),
         ],
         out_specs=pl.BlockSpec(memory_space=pltpu.VMEM),
+        scratch_shapes=[
+            pltpu.VMEM(resid.shape, jnp.float32),
+            pltpu.VMEM(resid.shape, jnp.float32),
+            pltpu.SemaphoreType.DMA,
+        ],
+        compiler_params=pltpu.CompilerParams(vmem_limit_bytes=VMEM_LIMIT),
         name="finish",
-    )(row_count, parts, residual_rows)
+    )(row_count, parts, resid)
 
 
 def to_all(x, ranks):
@@ -128,12 +139,13 @@
     gate = jnp.dot(gathered, gate_weight, preferred_element_type=jnp.float32)
     up = jnp.dot(gathered, up_weight, preferred_element_type=jnp.float32)
     hidden = (jax.nn.silu(gate) * up).astype(jnp.bfloat16)
-    hidden = to_all(hidden.T, ranks)
+    hidden, resid = lax.optimization_barrier((hidden.T, resid))
+    hidden = to_all(hidden, ranks)
 
     total = down_projection(hidden, down)
-    total, residual_rows, row_count = lax.optimization_barrier((total, residual_rows, row_count))
+    total, resid, row_count = lax.optimization_barrier((total, resid, row_count))
     parts = lax.all_to_all(total.reshape(ranks, own_rows, -1), "tp", 0, 0)
-    return finish(row_count, parts, residual_rows, groups, each)
+    return finish(row_count, parts, resid, groups, each)
 
 
 def solution(mesh):

time: 143 us -> 142 us (level)
  blocking collectives: 74.1 us -> 52.5 us
  waiting for transfers between devices: 23.4 us -> 35.8 us
  matrix products: 7.24 us -> 10.9 us
  starting transfers between devices: 6.6 us -> 10 us
    all_to_all x2 -> x1, blocking collectives: 58.7 us -> 37.1 us  [to_all(): lax.all_to_all(jnp.broadcast_to(x[None], (ranks, *x.shape)), 'tp', 0, 0)]
    all_to_all x0 -> x1, waiting for transfers between devices: none -> 21.3 us  [to_all(): lax.all_to_all(jnp.broadcast_to(x[None], (ranks, *x.shape)), 'tp', 0, 0)]
    all_gather x1, waiting for transfers between devices: 15.8 us -> 6.89 us  [shards(): down = lax.all_gather(mine, 'dp', axis=0, tiled=False)]
    dot_general x1, matrix products: 1.65 us -> 5.43 us  [shards(): up = jnp.dot(gathered, up_weight, preferred_element_type=jnp.float32)]
    all_to_all x0 -> x1, starting transfers between devices: none -> 3.71 us  [to_all(): lax.all_to_all(jnp.broadcast_to(x[None], (ranks, *x.shape)), 'tp', 0, 0)]
    pallas_call x1, Pallas kernels: 9.6 us -> 7.86 us  [down_projection(): pl.pallas_call(down_kernel, out_shape=jax.ShapeDtypeStruct((rows, feature...]
  transfers between devices with their start and end apart: 2 -> 3, of which waited for: 2 -> 3; matrix products, arithmetic and copies ran while one was open for 7% -> 11% of each run, Pallas kernels for 0% -> 0%
where the time goes in v6:
time: 142 us; the launch traced here: 141 us
  blocking collectives  52.5 us (37%)
  waiting for transfers between devices  35.8 us (25%)
  between operations  14.1 us (10%)
  matrix products  10.9 us (8%)
  Pallas kernels  10.9 us (8%)
  starting transfers between devices  10 us (7%)
  local copies, waits for them, and re-layouts  3.84 us (3%)
  other arithmetic  2.82 us (2%)
    all_to_all x1, blocking collectives, to_all(): lax.all_to_all(jnp.broadcast_to(x[None], (ranks, *x.shape)), 'tp', 0, 0)  37.1 us
    all_to_all x1, waiting for transfers between devices, to_all(): lax.all_to_all(jnp.broadcast_to(x[None], (ranks, *x.shape)), 'tp', 0, 0)  21.3 us
    all_to_all x1, blocking collectives, shards(): mine = lax.all_to_all(split, 'tp', 0, 0)  15.4 us
    pallas_call x1, Pallas kernels, down_projection(): pl.pallas_call(down_kernel, out_shape=jax.ShapeDtypeStruct((rows, feature...  7.86 us
    all_to_all x1, waiting for transfers between devices, shards(): parts = lax.all_to_all(total.reshape(ranks, own_rows, -1), 'tp', 0, 0)  7.6 us
    all_gather x1, waiting for transfers between devices, shards(): down = lax.all_gather(mine, 'dp', axis=0, tiled=False)  6.89 us
    all_to_all x1, starting transfers between devices, shards(): parts = lax.all_to_all(total.reshape(ranks, own_rows, -1), 'tp', 0, 0)  6.33 us
    dot_general x1, matrix products, shards(): up = jnp.dot(gathered, up_weight, preferred_element_type=jnp.float32)  5.43 us
  transfers between devices with their start and end apart: 3, of which 3 were waited for; matrix products, arithmetic and copies ran while one was open for 11% of the time, Pallas kernels for 0%

profile of v6, /device:TPU:1, one launch (start us, length us, event | category | flops | bytes accessed | tf_op | source)
XLA Modules:
  0.0 141.0 jit_solution(15079320763266141138)
XLA Ops:
  6.5 0.0 all-gather.3.cloned.1.call-start
  6.5 1.0 reshape.20
  7.6 15.4 %all_to_all.20 = bf16[16,16,640]{2,1,0:T(8,128)(2,1)} all-to-all(bf16[16,16,640]{2,1,0:T(8,128)(2,1)S(1)} %pad.4), channel_id=1, replica_groups=mesh['dp'=32,'tp'=16] {'tp'}, dimensions={0} | all-to-all | bytes 655360 | tf_op jit(solution)/shard_map/all_to_all | solution.py:134
  23.0 0.0 all-gather.3.cloned.1.call-update
  23.0 1.1 multiply_reduce_fusion
  24.1 1.0 multiply_convert_fusion
  25.1 0.0 copy-start.1
  25.1 1.4 broadcast_in_dim.4
  26.5 3.7 %all-to-all-start.1 = ((bf16[16,8,7168]{2,1,0:T(8,128)(2,1)}), bf16[16,8,7168]{2,1,0:T(8,128)(2,1)S(1)}, u32[]{:S(2)}, u32[]{:S(2)}) async-start(bf16[16,8,7168]{2,1,0:T(8,128)(2,1)} %broadcast_in_dim.4), calls=%async_computation.1 | async-start | bytes 3670016 | tf_op jit(solution)/shard_map/all_to_all | solution.py:123
  30.3 0.0 copy-done.1
  30.3 0.7 convert_element_type.12.resid_ref
  31.0 21.3 %all-to-all-done.1 = bf16[16,8,7168]{2,1,0:T(8,128)(2,1)S(1)} async-done(((bf16[16,8,7168]{2,1,0:T(8,128)(2,1)}), bf16[16,8,7168]{2,1,0:T(8,128)(2,1)S(1)}, u32[]{:S(2)}, u32[]{:S(2)}) %all-to-all-start.1) | async-done | bytes 1835040 | tf_op jit(solution)/shard_map/all_to_all | solution.py:123
  52.3 5.4 %fusion.4 = f32[640,128]{0,1:T(8,128)S(1)} fusion(bf16[7168,640]{1,0:T(8,128)(2,1)} %param.8, bf16[16,8,7168]{2,1,0:T(8,128)(2,1)S(1)} %all-to-all-done.1), kind=kOutput, calls=%fused_computation.4 | convolution fusion | flops 1174405120 | bytes 11337728 | tf_op jit(solution)/shard_map/dot_general | solution.py:139
  57.7 5.4 %fusion.13 = bf16[640,128]{0,1:T(8,128)(2,1)S(1)} fusion(bf16[7168,640]{1,0:T(8,128)(2,1)} %param.9, bf16[16,8,7168]{2,1,0:T(8,128)(2,1)S(1)} %all-to-all-done.1, f32[640,128]{0,1:T(8,128)S(1)} %fusion.4), kind=kOutput, calls=%fused_computation.7 | convolution fusion | flops 1174896640 | bytes 11501568 | tf_op jit(solution)/shard_map/dot_general | solution.py:140
  63.2 0.2 copy.9
  63.3 0.5 broadcast_in_dim.5
  63.9 37.1 %all_to_all.21.hidden_ref = bf16[16,640,128]{2,1,0:T(8,128)(2,1)} all-to-all(bf16[16,640,128]{2,1,0:T(8,128)(2,1)S(1)} %broadcast_in_dim.5), channel_id=1, replica_groups=mesh['dp'=32,'tp'=16] {'tp'}, dimensions={0} | all-to-all | bytes 5242880 | tf_op jit(solution)/shard_map/all_to_all | solution.py:123
  101.0 6.9 %all-gather.3.cloned.1.call-done = bf16[512,16,640]{2,1,0:T(8,128)(2,1)} async-done(((bf16[16,16,640]{2,1,0:T(8,128)(2,1)}), bf16[512,16,640]{2,1,0:T(8,128)(2,1)}) %all-gather.3.cloned.1.call-update) | async-done | bytes 10485776 | tf_op jit(solution)/shard_map/all_gather | solution.py:135
  107.9 7.9 %down_projection.1 = f32[128,512]{1,0:T(8,128)} custom-call(bf16[16,640,128]{2,1,0:T(8,128)(2,1)} %all_to_all.21.hidden_ref, bf16[32,16,16,640]{3,2,1,0:T(8,128)(2,1)} %bitcast.26), custom_call_target="tpu_custom_call" | custom-call | flops 1342177280 | bytes 13107200 | tf_op jit(solution)/shard_map/down_projection/pallas_call | solution.py:47
  115.7 6.3 %all-to-all-start.3 = ((f32[16,8,512]{2,1,0:T(8,128)}), f32[16,8,512]{2,1,0:T(8,128)S(1)}, u32[]{:S(2)}, u32[]{:S(2)}) async-start(f32[16,8,512]{2,1,0:T(8,128)} %bitcast.27), calls=%async_computation.3 | async-start | bytes 524288 | tf_op jit(solution)/shard_map/all_to_all | solution.py:147
  122.7 7.6 %all-to-all-done.3.parts_ref = f32[16,8,512]{2,1,0:T(8,128)S(1)} async-done(((f32[16,8,512]{2,1,0:T(8,128)}), f32[16,8,512]{2,1,0:T(8,128)S(1)}, u32[]{:S(2)}, u32[]{:S(2)}) %all-to-all-start.3) | async-done | bytes 262176 | tf_op jit(solution)/shard_map/all_to_all | solution.py:147
  130.3 0.0 copy-start
  130.3 0.7 copy-done
  131.0 3.1 %finish.1 = bf16[8,7168]{1,0:T(8,128)(2,1)} custom-call(s32[1]{0:T(128)S(6)} %copy.10.count_ref, f32[16,8,512]{2,1,0:T(8,128)} %copy-done, f32[8,7168]{1,0:T(8,128)} %convert_element_type.12.resid_ref), custom_call_target="tpu_custom_call" | custom-call | tf_op jit(solution)/shard_map/finish/pallas_call | solution.py:103
  (2 shorter events, 0.0 us)
Async XLA Ops:
  6.5 101.3 %all-gather.3.cloned.1.call-start = ((), (), s32[]{:S(2)}) async-start(), calls=%async_computation.4 | async-start | bytes 10813440 | tf_op jit(solution)/shard_map/all_gather | solution.py:135
  25.1 5.1 %copy-start.1 = (bf16[8,7168]{1,0:T(8,128)(2,1)S(1)}, bf16[8,7168]{1,0:T(8,128)(2,1)}, u32[]{:S(2)}) copy-start(bf16[8,7168]{1,0:T(8,128)(2,1)} %param.6) | copy-start | bytes 344068
  26.5 25.8 %all-to-all-start.1 = ((bf16[16,8,7168]{2,1,0:T(8,128)(2,1)}), bf16[16,8,7168]{2,1,0:T(8,128)(2,1)S(1)}, u32[]{:S(2)}, u32[]{:S(2)}) async-start(bf16[16,8,7168]{2,1,0:T(8,128)(2,1)} %broadcast_in_dim.4), calls=%async_computation.1 | async-start | bytes 3670016 | tf_op jit(solution)/shard_map/all_to_all | solution.py:123
  115.7 14.6 %all-to-all-start.3 = ((f32[16,8,512]{2,1,0:T(8,128)}), f32[16,8,512]{2,1,0:T(8,128)S(1)}, u32[]{:S(2)}, u32[]{:S(2)}) async-start(f32[16,8,512]{2,1,0:T(8,128)} %bitcast.27), calls=%async_computation.3 | async-start | bytes 524288 | tf_op jit(solution)/shard_map/all_to_all | solution.py:147
  130.3 0.7 copy-start
Sparse Core Ops, SparseCore 0:
  23.2 84.6 all-gather.2

commit v7 on v6

--- a/solution.py
+++ b/solution.py
@@ -63,12 +63,10 @@
     )(hidden, down)
 
 
-def finish_kernel(groups, each, count_ref, parts_ref, resid_ref, out_ref, resid, ffn, sem):
-    copy = pltpu.make_async_copy(resid_ref, resid, sem)
+def finish_kernel(groups, each, parts_ref, own_ref, out_ref, own, ffn, sem):
+    copy = pltpu.make_async_copy(own_ref, own, sem)
     copy.start()
     ranks, rows = parts_ref.shape[:2]
-    slots = lax.broadcasted_iota(jnp.int32, (rows, LANES), 0)
-    live = (slots < count_ref[0]).astype(jnp.float32)
     lane = lax.broadcasted_iota(jnp.int32, (rows, LANES), 1)
     tiles = {}
 
@@ -94,29 +92,26 @@
                 ffn[:, done * LANES : (done + 1) * LANES] = tiles.pop(done)
                 done += 1
     copy.wait()
+    live = own[:, done * LANES :]
     for i in range(done):
         part = slice(i * LANES, (i + 1) * LANES)
-        out_ref[:, part] = (live * (resid[:, part] + ffn[:, part])).astype(out_ref.dtype)
+        out_ref[:, part] = (live * (own[:, part] + ffn[:, part])).astype(out_ref.dtype)
 
 
-def finish(row_count, parts, resid, groups, each):
+def finish(parts, own, groups, each):
+    rows, width = own.shape[0], own.shape[1] - LANES
     return pl.pallas_call(
         functools.partial(finish_kernel, groups, each),
-        out_shape=jax.ShapeDtypeStruct(resid.shape, jnp.bfloat16),
-        in_specs=[
-            pl.BlockSpec(memory_space=pltpu.SMEM),
-            pl.BlockSpec(memory_space=pltpu.VMEM),
-            pl.BlockSpec(memory_space=pl.ANY),
-        ],
+        out_shape=jax.ShapeDtypeStruct((rows, width), jnp.bfloat16),
+        in_specs=[pl.BlockSpec(memory_space=pltpu.VMEM), pl.BlockSpec(memory_space=pl.ANY)],
         out_specs=pl.BlockSpec(memory_space=pltpu.VMEM),
         scratch_shapes=[
-            pltpu.VMEM(resid.shape, jnp.float32),
-            pltpu.VMEM(resid.shape, jnp.float32),
+            pltpu.VMEM(own.shape, jnp.float32),
+            pltpu.VMEM((rows, width), jnp.float32),
             pltpu.SemaphoreType.DMA,
         ],
-        compiler_params=pltpu.CompilerParams(vmem_limit_bytes=VMEM_LIMIT),
         name="finish",
-    )(row_count, parts, resid)
+    )(parts, own)
 
 
 def to_all(x, ranks):
@@ -136,16 +131,18 @@
 
     normed, mine = lax.optimization_barrier((normalize(resid, norm_gain), mine))
     gathered = to_all(normed, ranks).reshape(ranks * own_rows, width)
+    gathered, residual_rows, row_count = lax.optimization_barrier((gathered, residual_rows, row_count))
     gate = jnp.dot(gathered, gate_weight, preferred_element_type=jnp.float32)
     up = jnp.dot(gathered, up_weight, preferred_element_type=jnp.float32)
     hidden = (jax.nn.silu(gate) * up).astype(jnp.bfloat16)
-    hidden, resid = lax.optimization_barrier((hidden.T, resid))
+    live = lax.broadcasted_iota(jnp.int32, (own_rows, LANES), 0) < row_count[0]
+    own = jnp.concatenate([residual_rows.astype(jnp.float32), live.astype(jnp.float32)], axis=1)
+    hidden, own = lax.optimization_barrier((hidden.T, own))
     hidden = to_all(hidden, ranks)
 
     total = down_projection(hidden, down)
-    total, resid, row_count = lax.optimization_barrier((total, resid, row_count))
     parts = lax.all_to_all(total.reshape(ranks, own_rows, -1), "tp", 0, 0)
-    return finish(row_count, parts, resid, groups, each)
+    return finish(parts, own, groups, each)
 
 
 def solution(mesh):

time: 142 us -> 141 us (level)
  blocking collectives: 52.5 us -> 67.2 us
  starting transfers between devices: 10 us -> 3.71 us
  waiting for transfers between devices: 35.8 us -> 30.3 us
  matrix products: 10.9 us -> 7.27 us
    all_to_all x0 -> x1, blocking collectives: none -> 14.9 us  [shards(): parts = lax.all_to_all(total.reshape(ranks, own_rows, -1), 'tp', 0, 0)]
    all_to_all x1 -> x0, waiting for transfers between devices: 7.6 us -> none  [shards(): parts = lax.all_to_all(total.reshape(ranks, own_rows, -1), 'tp', 0, 0)]
    all_to_all x1 -> x0, starting transfers between devices: 6.33 us -> none  [shards(): parts = lax.all_to_all(total.reshape(ranks, own_rows, -1), 'tp', 0, 0)]
    dot_general x1, matrix products: 5.43 us -> 1.69 us  [shards(): up = jnp.dot(gathered, up_weight, preferred_element_type=jnp.float32)]
    all_gather x1, waiting for transfers between devices: 6.89 us -> 8.87 us  [shards(): down = lax.all_gather(mine, 'dp', axis=0, tiled=False)]
  transfers between devices with their start and end apart: 3 -> 2, of which waited for: 3 -> 2; matrix products, arithmetic and copies ran while one was open for 11% -> 9% of each run, Pallas kernels for 0% -> 0%
where the time goes in v7:
time: 141 us; the launch traced here: 140 us
  blocking collectives  67.2 us (48%)
  waiting for transfers between devices  30.3 us (21%)
  between operations  14.2 us (10%)
  Pallas kernels  10.9 us (8%)
  matrix products  7.27 us (5%)
  local copies, waits for them, and re-layouts  4.12 us (3%)
  starting transfers between devices  3.71 us (3%)
  other arithmetic  2.8 us (2%)
    all_to_all x1, blocking collectives, to_all(): lax.all_to_all(jnp.broadcast_to(x[None], (ranks, *x.shape)), 'tp', 0, 0)  36.9 us
    all_to_all x1, waiting for transfers between devices, to_all(): lax.all_to_all(jnp.broadcast_to(x[None], (ranks, *x.shape)), 'tp', 0, 0)  21.4 us
    all_to_all x1, blocking collectives, shards(): mine = lax.all_to_all(split, 'tp', 0, 0)  15.4 us
    all_to_all x1, blocking collectives, shards(): parts = lax.all_to_all(total.reshape(ranks, own_rows, -1), 'tp', 0, 0)  14.9 us
    all_gather x1, waiting for transfers between devices, shards(): down = lax.all_gather(mine, 'dp', axis=0, tiled=False)  8.87 us
    pallas_call x1, Pallas kernels, down_projection(): pl.pallas_call(down_kernel, out_shape=jax.ShapeDtypeStruct((rows, feature...  7.86 us
    dot_general x1, matrix products, shards(): gate = jnp.dot(gathered, gate_weight, preferred_element_type=jnp.float32)  5.58 us
    all_to_all x1, starting transfers between devices, to_all(): lax.all_to_all(jnp.broadcast_to(x[None], (ranks, *x.shape)), 'tp', 0, 0)  3.71 us
  transfers between devices with their start and end apart: 2, of which 2 were waited for; matrix products, arithmetic and copies ran while one was open for 9% of the time, Pallas kernels for 0%

profile of v7, /device:TPU:1, one launch (start us, length us, event | category | flops | bytes accessed | tf_op | source)
XLA Modules:
  0.0 140.5 jit_solution(18136534902689470048)
XLA Ops:
  6.5 1.0 reshape.20
  7.6 15.4 %all_to_all.20 = bf16[16,16,640]{2,1,0:T(8,128)(2,1)} all-to-all(bf16[16,16,640]{2,1,0:T(8,128)(2,1)S(1)} %pad.4), channel_id=1, replica_groups=mesh['dp'=32,'tp'=16] {'tp'}, dimensions={0} | all-to-all | bytes 655360 | tf_op jit(solution)/shard_map/all_to_all | solution.py:129
  23.0 0.0 all-gather.3.cloned.1.call-update
  23.0 1.1 fusion.2
  24.1 1.0 fusion.4
  25.1 0.0 copy-start
  25.1 1.4 broadcast_in_dim.4
  26.5 3.7 %all-to-all-start.1 = ((bf16[16,8,7168]{2,1,0:T(8,128)(2,1)}), bf16[16,8,7168]{2,1,0:T(8,128)(2,1)S(1)}, u32[]{:S(2)}, u32[]{:S(2)}) async-start(bf16[16,8,7168]{2,1,0:T(8,128)(2,1)} %broadcast_in_dim.4), calls=%async_computation.1 | async-start | bytes 3670016 | tf_op jit(solution)/shard_map/all_to_all | solution.py:118
  30.9 21.4 %all-to-all-done.1 = bf16[16,8,7168]{2,1,0:T(8,128)(2,1)S(1)} async-done(((bf16[16,8,7168]{2,1,0:T(8,128)(2,1)}), bf16[16,8,7168]{2,1,0:T(8,128)(2,1)S(1)}, u32[]{:S(2)}, u32[]{:S(2)}) %all-to-all-start.1) | async-done | bytes 1835040 | tf_op jit(solution)/shard_map/all_to_all | solution.py:118
  52.3 0.0 slice-start.1
  52.3 0.0 slice-start.2
  52.3 5.6 %convolution_bitcast_fusion.1 = f32[640,128]{0,1:T(8,128)S(1)} fusion(bf16[128,7168]{1,0:T(8,128)(2,1)S(1)} %bitcast.18, bf16[7168,640]{1,0:T(8,128)(2,1)} %param.8), kind=kOutput, calls=%fused_computation.1 | convolution fusion | flops 1174405120 | bytes 11337728 | tf_op jit(solution)/shard_map/dot_general | solution.py:135
  57.9 0.8 slice-done.1
  58.7 0.1 slice-done.2
  58.8 1.7 %fusion.1 = bf16[640,128]{0,1:T(8,128)(2,1)S(1)} fusion(bf16[128,7168]{1,0:T(8,128)(2,1)S(1)} %bitcast.19, bf16[7168,640]{1,0:T(8,128)(2,1)S(1)} %bitcast.21, f32[640,128]{0,1:T(8,128)S(1)} %convolution_bitcast_fusion.1), kind=kOutput, calls=%fused_computation.3 | convolution fusion | flops 1174896640 | bytes 11501568 | tf_op jit(solution)/shard_map/dot_general | solution.py:136
  60.5 0.1 iota.7
  60.6 0.7 pad_maximum_fusion.own_ref
  61.3 0.2 copy.9
  61.5 0.5 broadcast_in_dim.5
  62.0 36.9 %all_to_all.21.hidden_ref = bf16[16,640,128]{2,1,0:T(8,128)(2,1)} all-to-all(bf16[16,640,128]{2,1,0:T(8,128)(2,1)S(1)} %broadcast_in_dim.5), channel_id=1, replica_groups=mesh['dp'=32,'tp'=16] {'tp'}, dimensions={0} | all-to-all | bytes 5242880 | tf_op jit(solution)/shard_map/all_to_all | solution.py:118
  98.9 8.9 %all-gather.3.cloned.1.call-done = bf16[512,16,640]{2,1,0:T(8,128)(2,1)} async-done(((bf16[16,16,640]{2,1,0:T(8,128)(2,1)}), bf16[512,16,640]{2,1,0:T(8,128)(2,1)}) %all-gather.3.cloned.1.call-update) | async-done | bytes 10485776 | tf_op jit(solution)/shard_map/all_gather | solution.py:130
  107.8 7.9 %down_projection.1 = f32[128,512]{1,0:T(8,128)} custom-call(bf16[16,640,128]{2,1,0:T(8,128)(2,1)} %all_to_all.21.hidden_ref, bf16[32,16,16,640]{3,2,1,0:T(8,128)(2,1)} %bitcast.22), custom_call_target="tpu_custom_call" | custom-call | flops 1342177280 | bytes 13107200 | tf_op jit(solution)/shard_map/down_projection/pallas_call | solution.py:47
  115.6 14.9 %all_to_all.22.parts_ref = f32[16,8,512]{2,1,0:T(8,128)} all-to-all(f32[16,8,512]{2,1,0:T(8,128)} %bitcast.23), channel_id=1, replica_groups=mesh['dp'=32,'tp'=16] {'tp'}, dimensions={0} | all-to-all | bytes 524288 | tf_op jit(solution)/shard_map/all_to_all | solution.py:144
  130.5 3.1 %finish.1 = bf16[8,7168]{1,0:T(8,128)(2,1)} custom-call(f32[16,8,512]{2,1,0:T(8,128)} %all_to_all.22.parts_ref, f32[8,7296]{1,0:T(8,128)} %pad_maximum_fusion.own_ref), custom_call_target="tpu_custom_call" | custom-call | tf_op jit(solution)/shard_map/finish/pallas_call | solution.py:103
  (9 shorter events, 0.1 us)
Async XLA Ops:
  6.5 101.2 %all-gather.3.cloned.1.call-start = ((), (), s32[]{:S(2)}) async-start(), calls=%async_computation.4 | async-start | bytes 10813440 | tf_op jit(solution)/shard_map/all_gather | solution.py:130
  25.1 27.2 %copy-start = (bf16[8,7168]{1,0:T(8,128)(2,1)S(1)}, bf16[8,7168]{1,0:T(8,128)(2,1)}, u32[]{:S(2)}) copy-start(bf16[8,7168]{1,0:T(8,128)(2,1)} %param.6) | copy-start | bytes 344068
  26.5 25.8 %all-to-all-start.1 = ((bf16[16,8,7168]{2,1,0:T(8,128)(2,1)}), bf16[16,8,7168]{2,1,0:T(8,128)(2,1)S(1)}, u32[]{:S(2)}, u32[]{:S(2)}) async-start(bf16[16,8,7168]{2,1,0:T(8,128)(2,1)} %broadcast_in_dim.4), calls=%async_computation.1 | async-start | bytes 3670016 | tf_op jit(solution)/shard_map/all_to_all | solution.py:118
  52.3 5.6 %slice-start = ((s8[9175040]{0:T(1024)(128)(4,1)}), s8[4194304]{0:T(1024)(128)(4,1)S(1)}, s32[]{:S(2)}) async-start(s8[9175040]{0:T(1024)(128)(4,1)} %bitcast.20), calls=%async_computation.5 | async-start | bytes 8388608
  52.3 6.4 %slice-start.1 = ((s8[9175040]{0:T(1024)(128)(4,1)}), s8[4194304]{0:T(1024)(128)(4,1)S(1)}, s32[]{:S(2)}) async-start(s8[9175040]{0:T(1024)(128)(4,1)} %bitcast.20), calls=%async_computation.6 | async-start | bytes 8388608
  52.3 6.5 %slice-start.2 = ((s8[9175040]{0:T(1024)(128)(4,1)}), s8[786432]{0:T(1024)(128)(4,1)S(1)}, s32[]{:S(2)}) async-start(s8[9175040]{0:T(1024)(128)(4,1)} %bitcast.20), calls=%async_computation.7 | async-start | bytes 1572864
Sparse Core Ops, SparseCore 0:
  23.2 84.5 all-gather.2

commit v8 on v5

--- a/solution.py
+++ b/solution.py
@@ -9,7 +9,8 @@
 
 LANES = 128
 PADDED = 16
-STEP = 2
+CORES = 2
+CHUNK = 8
 
 
 def normalize(resid, norm_gain):
@@ -17,49 +18,55 @@
     return (resid * scale * norm_gain[None, :]).astype(jnp.bfloat16)
 
 
-def down_kernel(hidden_ref, down_ref, out_ref, total_ref):
-    step = pl.program_id(0)
-    features, rows = total_ref.shape
-    units = down_ref.shape[3]
-    block = jnp.concatenate([down_ref[:, i].reshape(features, units) for i in range(STEP)], axis=1)
-    hidden = hidden_ref[...].reshape(STEP * units, rows)
-    terms = jnp.dot(block, hidden, preferred_element_type=jnp.float32)
-
-    @pl.when(step == 0)
-    def _():
-        total_ref[...] = terms
-
-    @pl.when(step > 0)
-    def _():
-        total_ref[...] += terms
-
-    @pl.when(step == pl.num_programs(0) - 1)
-    def _():
-        out_ref[...] = total_ref[...].T
+def down_kernel(hidden_ref, other_ref, down_ref, out_ref, other_out_ref, held, sems):
+    chips, ranks, padded, units = held.shape
+    rows = hidden_ref.shape[2]
+    copies = []
+    for i in range(chips // CHUNK):
+        part = pl.ds(i * CHUNK, CHUNK)
+        copy = pltpu.make_async_copy(down_ref.at[part], held.at[part], sems.at[i])
+        copy.start()
+        copies.append(copy)
+    features = CHUNK * padded
+    for i, copy in enumerate(copies):
+        copy.wait()
+        total = None
+        for j in range(0, ranks, 2):
+            block = jnp.concatenate(
+                [held[i * CHUNK : (i + 1) * CHUNK, k].reshape(features, units) for k in (j, j + 1)], axis=1
+            )
+            hidden = jnp.concatenate(
+                [ref[j : j + 2].reshape(2 * units, rows) for ref in (hidden_ref, other_ref)], axis=1
+            )
+            terms = jnp.dot(block, hidden, preferred_element_type=jnp.float32)
+            total = terms if total is None else total + terms
+        part = slice(i * features, (i + 1) * features)
+        out_ref[:, part] = total[:, :rows].T
+        other_out_ref[:, part] = total[:, rows:].T
 
 
-def down_projection(hidden, down):
+def down_projection(hidden, other, down):
     ranks, units, rows = hidden.shape
-    groups = down.shape[0]
-    features = groups * PADDED
+    chips = down.shape[0]
+    features = chips * PADDED
+    in_vmem = pl.BlockSpec(memory_space=pltpu.VMEM)
     return pl.pallas_call(
         down_kernel,
-        grid=(ranks // STEP,),
-        out_shape=jax.ShapeDtypeStruct((rows, features), jnp.float32),
-        in_specs=[
-            pl.BlockSpec((STEP, units, rows), lambda i: (i, 0, 0)),
-            pl.BlockSpec((groups, STEP, PADDED, units), lambda i: (0, i, 0, 0)),
+        out_shape=[jax.ShapeDtypeStruct((rows, features), jnp.float32)] * 2,
+        in_specs=[in_vmem, in_vmem, pl.BlockSpec(memory_space=pl.ANY)],
+        out_specs=[in_vmem, in_vmem],
+        scratch_shapes=[
+            pltpu.VMEM(down.shape, jnp.bfloat16),
+            pltpu.SemaphoreType.DMA((chips // CHUNK,)),
         ],
-        out_specs=pl.BlockSpec((rows, features), lambda i: (0, 0)),
-        scratch_shapes=[pltpu.VMEM((features, rows), jnp.float32)],
         compiler_params=pltpu.CompilerParams(vmem_limit_bytes=56 * 1024 * 1024),
         cost_estimate=pl.CostEstimate(
-            flops=2 * rows * ranks * units * features,
-            bytes_accessed=2 * ranks * units * (features + rows),
+            flops=4 * rows * ranks * units * features,
+            bytes_accessed=2 * ranks * units * (features + 2 * rows),
             transcendentals=0,
         ),
         name="down_projection",
-    )(hidden, down)
+    )(hidden, other, down)
 
 
 def finish_kernel(groups, each, count_ref, parts_ref, resid_ref, out_ref):
@@ -67,6 +74,14 @@
     slots = lax.broadcasted_iota(jnp.int32, (rows, LANES), 0)
     live = (slots < count_ref[0]).astype(jnp.float32)
     lane = lax.broadcasted_iota(jnp.int32, (rows, LANES), 1)
+    first_core = lax.rem(lax.axis_index("dp"), CORES) == 0
+    half = groups // CORES * PADDED
+    held = {}
+    for rank in range(ranks):
+        for at in range(0, half, LANES):
+            mine, other = (parts_ref[rank, :, i : i + LANES] for i in (at, half + at))
+            held[rank, 0, at] = jnp.where(first_core, mine, other)
+            held[rank, 1, at] = jnp.where(first_core, other, mine)
     tiles = {}
 
     def put(tile, start, stop, value):
@@ -77,12 +92,11 @@
 
     done = 0
     for group in range(groups):
-        source = group * PADDED
+        source = group // CORES * PADDED
         for rank in range(ranks):
             target = (group * ranks + rank) * each
             tile, start = divmod(target, LANES)
-            first = source // LANES * LANES
-            value = parts_ref[rank, :, first : first + LANES]
+            value = held[rank, group % CORES, source // LANES * LANES]
             value = pltpu.roll(value, (start - source % LANES) % LANES, 1)
             put(tile, start, min(start + each, LANES), value)
             if start + each > LANES:
@@ -121,7 +135,8 @@
 
     split = jnp.pad(down_weight.T.reshape(ranks, each, units), ((0, 0), (0, PADDED - each), (0, 0)))
     mine = lax.all_to_all(split, "tp", 0, 0)
-    down = lax.all_gather(mine, "dp", axis=0, tiled=False)
+    same_core = [list(range(core, groups, CORES)) for core in range(CORES)]
+    down = lax.all_gather(mine, "dp", axis=0, tiled=False, axis_index_groups=same_core)
 
     normed, mine = lax.optimization_barrier((normalize(resid, norm_gain), mine))
     gathered = to_all(normed, ranks).reshape(ranks * own_rows, width)
@@ -130,7 +145,9 @@
     hidden = (jax.nn.silu(gate) * up).astype(jnp.bfloat16)
     hidden = to_all(hidden.T, ranks)
 
-    total = down_projection(hidden, down)
+    swap = [(i, i ^ 1) for i in range(groups)]
+    total, others = down_projection(hidden, lax.ppermute(hidden, "dp", swap), down)
+    total = jnp.concatenate([total, lax.ppermute(others, "dp", swap)], axis=1)
     total, residual_rows, row_count = lax.optimization_barrier((total, residual_rows, row_count))
     parts = lax.all_to_all(total.reshape(ranks, own_rows, -1), "tp", 0, 0)
     return finish(row_count, parts, residual_rows, groups, each)

time: 143 us -> 147 us (1.028)
  starting transfers between devices: 6.6 us -> 28.9 us
  blocking collectives: 74.1 us -> 57.6 us
  waiting for transfers between devices: 23.4 us -> 20.1 us
  other arithmetic: 2.08 us -> 3.7 us
    all_gather x1, waiting for transfers between devices: 15.8 us -> 0.01 us  [shards(): lax.all_gather(mine, 'dp', axis=0, tiled=False, axis_index_groups=same_core)]
    all_to_all x1 -> x0, blocking collectives: 15.4 us -> none  [shards(): mine = lax.all_to_all(split, 'tp', 0, 0)]
    ppermute x0 -> x2, starting transfers between devices: none -> 14.7 us  [the longest x1 7.68 us: shards(): lax.ppermute(hidden, 'dp', swap)]
    all_to_all x0 -> x1, starting transfers between devices: none -> 7.58 us  [shards(): mine = lax.all_to_all(split, 'tp', 0, 0)]
    all_to_all x0 -> x1, waiting for transfers between devices: none -> 6.78 us  [shards(): mine = lax.all_to_all(split, 'tp', 0, 0)]
    ppermute x0 -> x2, waiting for transfers between devices: none -> 5.82 us  [the longest x1 4.65 us: shards(): lax.ppermute(hidden, 'dp', swap)]
    concatenate x0 -> x1, other arithmetic: none -> 1.62 us  [shards(): total = jnp.concatenate([total, lax.ppermute(others, 'dp', swap)], axis=1)]
  transfers between devices with their start and end apart: 2 -> 5, of which waited for: 2 -> 4; matrix products, arithmetic and copies ran while one was open for 7% -> 7% of each run, Pallas kernels for 0% -> 0%
where the time goes in v8:
time: 147 us; the launch traced here: 146 us
  blocking collectives  57.6 us (39%)
  starting transfers between devices  28.9 us (20%)
  waiting for transfers between devices  20.1 us (14%)
  between operations  14.2 us (10%)
  Pallas kernels  10.4 us (7%)
  matrix products  7.16 us (5%)
  local copies, waits for them, and re-layouts  4.09 us (3%)
  other arithmetic  3.7 us (3%)
    all_to_all x2, blocking collectives, to_all(): lax.all_to_all(jnp.broadcast_to(x[None], (ranks, *x.shape)), 'tp', 0, 0)  57.6 us
    pallas_call x1, Pallas kernels, down_projection(): pl.pallas_call(down_kernel, out_shape=[jax.ShapeDtypeStruct((rows, featur...  8.15 us
    ppermute x1, starting transfers between devices, shards(): lax.ppermute(hidden, 'dp', swap)  7.68 us
    all_to_all x1, starting transfers between devices, shards(): mine = lax.all_to_all(split, 'tp', 0, 0)  7.58 us
    all_to_all x1, waiting for transfers between devices, shards(): parts = lax.all_to_all(total.reshape(ranks, own_rows, -1), 'tp', 0, 0)  7.48 us
    ppermute x1, starting transfers between devices, shards(): total = jnp.concatenate([total, lax.ppermute(others, 'dp', swap)], axis=1)  6.98 us
    all_to_all x1, waiting for transfers between devices, shards(): mine = lax.all_to_all(split, 'tp', 0, 0)  6.78 us
    all_to_all x1, starting transfers between devices, shards(): parts = lax.all_to_all(total.reshape(ranks, own_rows, -1), 'tp', 0, 0)  6.64 us
  transfers between devices with their start and end apart: 5, of which 4 were waited for; matrix products, arithmetic and copies ran while one was open for 7% of the time, Pallas kernels for 0%

profile of v8, /device:TPU:1, one launch (start us, length us, event | category | flops | bytes accessed | tf_op | source)
XLA Modules:
  0.0 146.2 jit_solution(16333310910606202859)
XLA Ops:
  6.5 1.0 reshape.20
  7.6 0.8 pad.4
  8.3 7.6 %all-to-all-start = ((bf16[16,16,640]{2,1,0:T(8,128)(2,1)}), bf16[16,16,640]{2,1,0:T(8,128)(2,1)S(1)}, u32[]{:S(2)}, u32[]{:S(2)}) async-start(bf16[16,16,640]{2,1,0:T(8,128)(2,1)} %pad.4), calls=%async_computation | async-start | bytes 655360 | tf_op jit(solution)/shard_map/all_to_all | solution.py:137
  16.0 1.1 fusion.16
  17.1 6.8 %all-to-all-done = bf16[16,16,640]{2,1,0:T(8,128)(2,1)S(1)} async-done(((bf16[16,16,640]{2,1,0:T(8,128)(2,1)}), bf16[16,16,640]{2,1,0:T(8,128)(2,1)S(1)}, u32[]{:S(2)}, u32[]{:S(2)}) %all-to-all-start) | async-done | bytes 327712 | tf_op jit(solution)/shard_map/all_to_all | solution.py:137
  23.8 0.7 copy-done.1
  24.6 1.0 fusion.18
  25.6 0.2 broadcast_in_dim.4
  25.8 25.0 %all_to_all.20 = bf16[16,8,7168]{2,1,0:T(8,128)(2,1)S(1)} all-to-all(bf16[16,8,7168]{2,1,0:T(8,128)(2,1)S(1)} %broadcast_in_dim.4), channel_id=1, replica_groups=mesh['dp'=32,'tp'=16] {'tp'}, dimensions={0} | all-to-all | bytes 3670016 | tf_op jit(solution)/shard_map/all_to_all | solution.py:126
  50.8 5.5 %fusion.4 = f32[640,128]{0,1:T(8,128)S(1)} fusion(bf16[7168,640]{1,0:T(8,128)(2,1)} %param.8, bf16[16,8,7168]{2,1,0:T(8,128)(2,1)S(1)} %all_to_all.20), kind=kOutput, calls=%fused_computation.4 | convolution fusion | flops 1174405120 | bytes 11337728 | tf_op jit(solution)/shard_map/dot_general | solution.py:143
  56.3 1.7 %fusion.13 = bf16[640,128]{0,1:T(8,128)(2,1)S(1)} fusion(bf16[7168,640]{1,0:T(8,128)(2,1)S(1)} %bitcast.27, bf16[16,8,7168]{2,1,0:T(8,128)(2,1)S(1)} %all_to_all.20, f32[640,128]{0,1:T(8,128)S(1)} %fusion.4), kind=kOutput, calls=%fused_computation.7 | convolution fusion | flops 1174896640 | bytes 11501568 | tf_op jit(solution)/shard_map/dot_general | solution.py:144
  58.0 0.2 copy.9
  58.2 0.5 broadcast_in_dim.5
  58.7 32.6 %all_to_all.21.hidden_ref = bf16[16,640,128]{2,1,0:T(8,128)(2,1)S(1)} all-to-all(bf16[16,640,128]{2,1,0:T(8,128)(2,1)S(1)} %broadcast_in_dim.5), channel_id=1, replica_groups=mesh['dp'=32,'tp'=16] {'tp'}, dimensions={0} | all-to-all | bytes 5242880 | tf_op jit(solution)/shard_map/all_to_all | solution.py:126
  91.3 7.7 %collective-permute-start = (bf16[16,640,128]{2,1,0:T(8,128)(2,1)S(1)}, bf16[16,640,128]{2,1,0:T(8,128)(2,1)}, u32[]{:S(2)}, u32[]{:S(2)}) collective-permute-start(bf16[16,640,128]{2,1,0:T(8,128)(2,1)S(1)} %all_to_all.21.hidden_ref), channel_id=1, source_target_pairs={{0,16},{16,0},{32,48},{48,32},{64,80},{80,64},{96,112},{112,96},{1... | collective-permute-start | bytes 7864328 | tf_op jit(solution)/shard_map/ppermute | solution.py:149
  99.0 4.6 %collective-permute-done.other_ref = bf16[16,640,128]{2,1,0:T(8,128)(2,1)} collective-permute-done((bf16[16,640,128]{2,1,0:T(8,128)(2,1)S(1)}, bf16[16,640,128]{2,1,0:T(8,128)(2,1)}, u32[]{:S(2)}, u32[]{:S(2)}) %collective-permute-start) | collective-permute-done | bytes 2621472 | tf_op jit(solution)/shard_map/ppermute | solution.py:149
  103.7 8.2 %down_projection.1 = (f32[128,256]{1,0:T(8,128)}, f32[128,256]{1,0:T(8,128)}) custom-call(bf16[16,640,128]{2,1,0:T(8,128)(2,1)} %copy-done, bf16[16,640,128]{2,1,0:T(8,128)(2,1)} %collective-permute-done.other_ref, bf16[16,16,16,640]{3,2,1,0:T(8,128)(2,1)} %bitcast.28), custom_call_target="tpu_custom_call" | custom-call | flops 1342177280 | bytes 10485760 | tf_op jit(solution)/shard_map/down_projection/pallas_call | solution.py:53
  111.8 7.0 %collective-permute-start.1 = (f32[128,256]{1,0:T(8,128)}, f32[128,256]{1,0:T(8,128)S(1)}, u32[]{:S(2)}, u32[]{:S(2)}) collective-permute-start(f32[128,256]{1,0:T(8,128)} %get-tuple-element.13), channel_id=1, source_target_pairs={{0,16},{16,0},{32,48},{48,32},{64,80},{80,64},{96,112},{112,96},{1... | collective-permute-start | bytes 393224 | tf_op jit(solution)/shard_map/ppermute | solution.py:150
  118.8 1.2 collective-permute-done.1
  120.0 1.6 %pad_maximum_fusion = f32[128,512]{1,0:T(8,128)} fusion(f32[128,256]{1,0:T(8,128)S(1)} %collective-permute-done.1, f32[128,256]{1,0:T(8,128)} %get-tuple-element.12), kind=kLoop, calls=%fused_computation.10 | loop fusion | flops 65536 | bytes 524288 | tf_op jit(solution)/shard_map/concatenate | solution.py:150
  121.6 6.6 %all-to-all-start.3 = ((f32[16,8,512]{2,1,0:T(8,128)}), f32[16,8,512]{2,1,0:T(8,128)S(1)}, u32[]{:S(2)}, u32[]{:S(2)}) async-start(f32[16,8,512]{2,1,0:T(8,128)} %bitcast.5), calls=%async_computation.3 | async-start | bytes 524288 | tf_op jit(solution)/shard_map/all_to_all | solution.py:152
  128.9 7.5 %all-to-all-done.3.parts_ref = f32[16,8,512]{2,1,0:T(8,128)S(1)} async-done(((f32[16,8,512]{2,1,0:T(8,128)}), f32[16,8,512]{2,1,0:T(8,128)S(1)}, u32[]{:S(2)}, u32[]{:S(2)}) %all-to-all-start.3) | async-done | bytes 262176 | tf_op jit(solution)/shard_map/all_to_all | solution.py:152
  136.4 0.7 copy-done.2
  137.1 2.2 %finish.1 = bf16[8,7168]{1,0:T(8,128)(2,1)} custom-call(s32[1]{0:T(128)S(6)} %copy.10.count_ref, f32[16,8,512]{2,1,0:T(8,128)} %copy-done.2, bf16[8,7168]{1,0:T(8,128)(2,1)} %resid_ref), custom_call_target="tpu_custom_call" | custom-call | tf_op jit(solution)/shard_map/finish/pallas_call | solution.py:112
  (15 shorter events, 0.1 us)
Async XLA Ops:
  8.3 15.5 %all-to-all-start = ((bf16[16,16,640]{2,1,0:T(8,128)(2,1)}), bf16[16,16,640]{2,1,0:T(8,128)(2,1)S(1)}, u32[]{:S(2)}, u32[]{:S(2)}) async-start(bf16[16,16,640]{2,1,0:T(8,128)(2,1)} %pad.4), calls=%async_computation | async-start | bytes 655360 | tf_op jit(solution)/shard_map/all_to_all | solution.py:137
  15.9 87.7 %all-gather.3.cloned.1.call-start = ((), (), s32[]{:S(2)}) async-start(), calls=%async_computation.4 | async-start | bytes 5570560 | tf_op jit(solution)/shard_map/all_gather | solution.py:139
  23.8 0.7 copy-start.1
  25.8 30.5 %slice-start = ((s8[9175040]{0:T(1024)(128)(4,1)}), s8[4194304]{0:T(1024)(128)(4,1)S(1)}, s32[]{:S(2)}) async-start(s8[9175040]{0:T(1024)(128)(4,1)} %bitcast.26), calls=%async_computation.5 | async-start | bytes 8388608
  50.8 5.5 %slice-start.1 = ((s8[9175040]{0:T(1024)(128)(4,1)}), s8[4194304]{0:T(1024)(128)(4,1)S(1)}, s32[]{:S(2)}) async-start(s8[9175040]{0:T(1024)(128)(4,1)} %bitcast.26), calls=%async_computation.6 | async-start | bytes 8388608
  50.8 5.5 %slice-start.2 = ((s8[9175040]{0:T(1024)(128)(4,1)}), s8[786432]{0:T(1024)(128)(4,1)S(1)}, s32[]{:S(2)}) async-start(s8[9175040]{0:T(1024)(128)(4,1)} %bitcast.26), calls=%async_computation.7 | async-start | bytes 1572864
  91.3 12.3 %copy-start = (bf16[16,640,128]{2,1,0:T(8,128)(2,1)}, bf16[16,640,128]{2,1,0:T(8,128)(2,1)S(1)}, u32[]{:S(2)}) copy-start(bf16[16,640,128]{2,1,0:T(8,128)(2,1)S(1)} %all_to_all.21.hidden_ref) | copy-start | bytes 7864324
  91.3 12.3 %collective-permute-start = (bf16[16,640,128]{2,1,0:T(8,128)(2,1)S(1)}, bf16[16,640,128]{2,1,0:T(8,128)(2,1)}, u32[]{:S(2)}, u32[]{:S(2)}) collective-permute-start(bf16[16,640,128]{2,1,0:T(8,128)(2,1)S(1)} %all_to_all.21.hidden_ref), channel_id=1, source_target_pairs={{0,16},{16,0},{32,48},{48,32},{64,80},{80,64},{96,112},{112,96},{1... | collective-permute-start | bytes 7864328 | tf_op jit(solution)/shard_map/ppermute | solution.py:149
  111.8 8.2 %collective-permute-start.1 = (f32[128,256]{1,0:T(8,128)}, f32[128,256]{1,0:T(8,128)S(1)}, u32[]{:S(2)}, u32[]{:S(2)}) collective-permute-start(f32[128,256]{1,0:T(8,128)} %get-tuple-element.13), channel_id=1, source_target_pairs={{0,16},{16,0},{32,48},{48,32},{64,80},{80,64},{96,112},{112,96},{1... | collective-permute-start | bytes 393224 | tf_op jit(solution)/shard_map/ppermute | solution.py:150
  121.6 14.8 %all-to-all-start.3 = ((f32[16,8,512]{2,1,0:T(8,128)}), f32[16,8,512]{2,1,0:T(8,128)S(1)}, u32[]{:S(2)}, u32[]{:S(2)}) async-start(f32[16,8,512]{2,1,0:T(8,128)} %bitcast.5), calls=%async_computation.3 | async-start | bytes 524288 | tf_op jit(solution)/shard_map/all_to_all | solution.py:152
  136.4 0.7 copy-start.2
Sparse Core Ops, SparseCore 0:
  24.7 76.5 all-gather.2

commit v9 on v7

--- a/solution.py
+++ b/solution.py
@@ -10,7 +10,7 @@
 LANES = 128
 PADDED = 16
 CHUNK = 8
-VMEM_LIMIT = 56 * 1024 * 1024
+VMEM_LIMIT = 52 * 1024 * 1024
 
 
 def normalize(resid, norm_gain):
@@ -63,10 +63,9 @@
     )(hidden, down)
 
 
-def finish_kernel(groups, each, parts_ref, own_ref, out_ref, own, ffn, sem):
-    copy = pltpu.make_async_copy(own_ref, own, sem)
-    copy.start()
+def finish_kernel(groups, each, parts_ref, own_ref, out_ref):
     ranks, rows = parts_ref.shape[:2]
+    live = own_ref[:, out_ref.shape[1] :]
     lane = lax.broadcasted_iota(jnp.int32, (rows, LANES), 1)
     tiles = {}
 
@@ -89,13 +88,9 @@
             if start + each > LANES:
                 put(tile + 1, 0, start + each - LANES, value)
             while done < tile or (done in tiles and (done + 1) * LANES <= target + each):
-                ffn[:, done * LANES : (done + 1) * LANES] = tiles.pop(done)
+                part = slice(done * LANES, (done + 1) * LANES)
+                out_ref[:, part] = (live * (own_ref[:, part] + tiles.pop(done))).astype(out_ref.dtype)
                 done += 1
-    copy.wait()
-    live = own[:, done * LANES :]
-    for i in range(done):
-        part = slice(i * LANES, (i + 1) * LANES)
-        out_ref[:, part] = (live * (own[:, part] + ffn[:, part])).astype(out_ref.dtype)
 
 
 def finish(parts, own, groups, each):
@@ -103,13 +98,8 @@
     return pl.pallas_call(
         functools.partial(finish_kernel, groups, each),
         out_shape=jax.ShapeDtypeStruct((rows, width), jnp.bfloat16),
-        in_specs=[pl.BlockSpec(memory_space=pltpu.VMEM), pl.BlockSpec(memory_space=pl.ANY)],
+        in_specs=[pl.BlockSpec(memory_space=pltpu.VMEM)] * 2,
         out_specs=pl.BlockSpec(memory_space=pltpu.VMEM),
-        scratch_shapes=[
-            pltpu.VMEM(own.shape, jnp.float32),
-            pltpu.VMEM((rows, width), jnp.float32),
-            pltpu.SemaphoreType.DMA,
-        ],
         name="finish",
     )(parts, own)
 

time: 141 us -> 139 us (0.986)
  Pallas kernels: 10.9 us -> 9.4 us
where the time goes in v9:
time: 139 us
  blocking collectives  67 us (48%)
  waiting for transfers between devices  30.3 us (22%)
  between operations  14.1 us (10%)
  Pallas kernels  9.4 us (7%)
  matrix products  7.27 us (5%)
  local copies, waits for them, and re-layouts  4.12 us (3%)
  starting transfers between devices  3.71 us (3%)
  other arithmetic  2.8 us (2%)
    all_to_all x1, blocking collectives, to_all(): lax.all_to_all(jnp.broadcast_to(x[None], (ranks, *x.shape)), 'tp', 0, 0)  36.9 us
    all_to_all x1, waiting for transfers between devices, to_all(): lax.all_to_all(jnp.broadcast_to(x[None], (ranks, *x.shape)), 'tp', 0, 0)  21.4 us
    all_to_all x1, blocking collectives, shards(): mine = lax.all_to_all(split, 'tp', 0, 0)  15.4 us
    all_to_all x1, blocking collectives, shards(): parts = lax.all_to_all(total.reshape(ranks, own_rows, -1), 'tp', 0, 0)  14.7 us
    all_gather x1, waiting for transfers between devices, shards(): down = lax.all_gather(mine, 'dp', axis=0, tiled=False)  8.87 us
    pallas_call x1, Pallas kernels, down_projection(): pl.pallas_call(down_kernel, out_shape=jax.ShapeDtypeStruct((rows, feature...  7.13 us
    dot_general x1, matrix products, shards(): gate = jnp.dot(gathered, gate_weight, preferred_element_type=jnp.float32)  5.58 us
    all_to_all x1, starting transfers between devices, to_all(): lax.all_to_all(jnp.broadcast_to(x[None], (ranks, *x.shape)), 'tp', 0, 0)  3.71 us
  transfers between devices with their start and end apart: 2, of which 2 were waited for; matrix products, arithmetic and copies ran while one was open for 9% of the time, Pallas kernels for 0%

profile of v9, /device:TPU:1, one launch (start us, length us, event | category | flops | bytes accessed | tf_op | source)
XLA Modules:
  0.0 138.7 jit_solution(15785998582932142291)
XLA Ops:
  6.5 1.0 reshape.20
  7.6 15.4 %all_to_all.20 = bf16[16,16,640]{2,1,0:T(8,128)(2,1)} all-to-all(bf16[16,16,640]{2,1,0:T(8,128)(2,1)S(1)} %pad.4), channel_id=1, replica_groups=mesh['dp'=32,'tp'=16] {'tp'}, dimensions={0} | all-to-all | bytes 655360 | tf_op jit(solution)/shard_map/all_to_all | solution.py:119
  23.0 0.0 all-gather.3.cloned.1.call-update
  23.0 1.1 fusion.2
  24.1 1.0 fusion.4
  25.1 0.0 copy-start
  25.1 1.4 %broadcast_in_dim.4 = bf16[16,8,7168]{2,1,0:T(8,128)(2,1)} broadcast(bf16[8,7168]{1,0:T(8,128)(2,1)S(1)} %fusion.4), dimensions={1,2} | broadcast | bytes 1949696 | tf_op jit(solution)/shard_map/broadcast_in_dim | solution.py:108
  26.5 3.7 %all-to-all-start.1 = ((bf16[16,8,7168]{2,1,0:T(8,128)(2,1)}), bf16[16,8,7168]{2,1,0:T(8,128)(2,1)S(1)}, u32[]{:S(2)}, u32[]{:S(2)}) async-start(bf16[16,8,7168]{2,1,0:T(8,128)(2,1)} %broadcast_in_dim.4), calls=%async_computation.1 | async-start | bytes 3670016 | tf_op jit(solution)/shard_map/all_to_all | solution.py:108
  30.9 21.4 %all-to-all-done.1 = bf16[16,8,7168]{2,1,0:T(8,128)(2,1)S(1)} async-done(((bf16[16,8,7168]{2,1,0:T(8,128)(2,1)}), bf16[16,8,7168]{2,1,0:T(8,128)(2,1)S(1)}, u32[]{:S(2)}, u32[]{:S(2)}) %all-to-all-start.1) | async-done | bytes 1835040 | tf_op jit(solution)/shard_map/all_to_all | solution.py:108
  52.3 0.0 slice-start.1
  52.3 0.0 slice-start.2
  52.3 5.6 %convolution_bitcast_fusion.1 = f32[640,128]{0,1:T(8,128)S(1)} fusion(bf16[128,7168]{1,0:T(8,128)(2,1)S(1)} %bitcast.19, bf16[7168,640]{1,0:T(8,128)(2,1)} %param.8), kind=kOutput, calls=%fused_computation.1 | convolution fusion | flops 1174405120 | bytes 11337728 | tf_op jit(solution)/shard_map/dot_general | solution.py:125
  57.9 0.8 slice-done.1
  58.7 0.1 slice-done.2
  58.8 1.7 %fusion.1 = bf16[640,128]{0,1:T(8,128)(2,1)S(1)} fusion(bf16[128,7168]{1,0:T(8,128)(2,1)S(1)} %bitcast.20, bf16[7168,640]{1,0:T(8,128)(2,1)S(1)} %bitcast.22, f32[640,128]{0,1:T(8,128)S(1)} %convolution_bitcast_fusion.1), kind=kOutput, calls=%fused_computation.3 | convolution fusion | flops 1174896640 | bytes 11501568 | tf_op jit(solution)/shard_map/dot_general | solution.py:126
  60.5 0.1 iota.7
  60.6 0.7 pad_maximum_fusion.own_ref
  61.3 0.2 copy.9
  61.5 0.5 broadcast_in_dim.5
  62.0 36.9 %all_to_all.21.hidden_ref = bf16[16,640,128]{2,1,0:T(8,128)(2,1)} all-to-all(bf16[16,640,128]{2,1,0:T(8,128)(2,1)S(1)} %broadcast_in_dim.5), channel_id=1, replica_groups=mesh['dp'=32,'tp'=16] {'tp'}, dimensions={0} | all-to-all | bytes 5242880 | tf_op jit(solution)/shard_map/all_to_all | solution.py:108
  98.9 8.9 %all-gather.3.cloned.1.call-done = bf16[512,16,640]{2,1,0:T(8,128)(2,1)} async-done(((bf16[16,16,640]{2,1,0:T(8,128)(2,1)}), bf16[512,16,640]{2,1,0:T(8,128)(2,1)}) %all-gather.3.cloned.1.call-update) | async-done | bytes 10485776 | tf_op jit(solution)/shard_map/all_gather | solution.py:120
  107.8 7.1 %down_projection.1 = f32[128,512]{1,0:T(8,128)S(1)} custom-call(bf16[16,640,128]{2,1,0:T(8,128)(2,1)} %all_to_all.21.hidden_ref, bf16[32,16,16,640]{3,2,1,0:T(8,128)(2,1)} %bitcast.23), custom_call_target="tpu_custom_call" | custom-call | flops 1342177280 | bytes 13107200 | tf_op jit(solution)/shard_map/down_projection/pallas_call | solution.py:47
  114.9 14.7 %all_to_all.22.parts_ref = f32[16,8,512]{2,1,0:T(8,128)} all-to-all(f32[16,8,512]{2,1,0:T(8,128)S(1)} %bitcast.18), channel_id=1, replica_groups=mesh['dp'=32,'tp'=16] {'tp'}, dimensions={0} | all-to-all | bytes 524288 | tf_op jit(solution)/shard_map/all_to_all | solution.py:134
  129.6 2.3 %finish.1 = bf16[8,7168]{1,0:T(8,128)(2,1)} custom-call(f32[16,8,512]{2,1,0:T(8,128)} %all_to_all.22.parts_ref, f32[8,7296]{1,0:T(8,128)} %pad_maximum_fusion.own_ref), custom_call_target="tpu_custom_call" | custom-call | tf_op jit(solution)/shard_map/finish/pallas_call | solution.py:98
  (9 shorter events, 0.1 us)
Async XLA Ops:
  6.5 101.2 %all-gather.3.cloned.1.call-start = ((), (), s32[]{:S(2)}) async-start(), calls=%async_computation.4 | async-start | bytes 10813440 | tf_op jit(solution)/shard_map/all_gather | solution.py:120
  25.1 27.2 %copy-start = (bf16[8,7168]{1,0:T(8,128)(2,1)S(1)}, bf16[8,7168]{1,0:T(8,128)(2,1)}, u32[]{:S(2)}) copy-start(bf16[8,7168]{1,0:T(8,128)(2,1)} %param.6) | copy-start | bytes 344068
  26.5 25.8 %all-to-all-start.1 = ((bf16[16,8,7168]{2,1,0:T(8,128)(2,1)}), bf16[16,8,7168]{2,1,0:T(8,128)(2,1)S(1)}, u32[]{:S(2)}, u32[]{:S(2)}) async-start(bf16[16,8,7168]{2,1,0:T(8,128)(2,1)} %broadcast_in_dim.4), calls=%async_computation.1 | async-start | bytes 3670016 | tf_op jit(solution)/shard_map/all_to_all | solution.py:108
  52.3 5.6 %slice-start = ((s8[9175040]{0:T(1024)(128)(4,1)}), s8[4194304]{0:T(1024)(128)(4,1)S(1)}, s32[]{:S(2)}) async-start(s8[9175040]{0:T(1024)(128)(4,1)} %bitcast.21), calls=%async_computation.5 | async-start | bytes 8388608
  52.3 6.4 %slice-start.1 = ((s8[9175040]{0:T(1024)(128)(4,1)}), s8[4194304]{0:T(1024)(128)(4,1)S(1)}, s32[]{:S(2)}) async-start(s8[9175040]{0:T(1024)(128)(4,1)} %bitcast.21), calls=%async_computation.6 | async-start | bytes 8388608
  52.3 6.5 %slice-start.2 = ((s8[9175040]{0:T(1024)(128)(4,1)}), s8[786432]{0:T(1024)(128)(4,1)S(1)}, s32[]{:S(2)}) async-start(s8[9175040]{0:T(1024)(128)(4,1)} %bitcast.21), calls=%async_computation.7 | async-start | bytes 1572864
Sparse Core Ops, SparseCore 0:
  23.2 84.5 all-gather.2

commit v10 on v9

--- a/solution.py
+++ b/solution.py
@@ -10,7 +10,7 @@
 LANES = 128
 PADDED = 16
 CHUNK = 8
-VMEM_LIMIT = 52 * 1024 * 1024
+VMEM_LIMIT = 46 * 1024 * 1024
 
 
 def normalize(resid, norm_gain):
@@ -18,34 +18,56 @@
     return (resid * scale * norm_gain[None, :]).astype(jnp.bfloat16)
 
 
-def down_kernel(hidden_ref, down_ref, out_ref, held, sems):
-    groups, ranks, padded, units = held.shape
+def fetch_kernel(x_ref, out_ref, sem):
+    copy = pltpu.make_async_copy(x_ref, out_ref, sem)
+    copy.start()
+    copy.wait()
+
+
+def fetched(x):
+    return pl.pallas_call(
+        fetch_kernel,
+        out_shape=jax.ShapeDtypeStruct(x.shape, x.dtype),
+        in_specs=[pl.BlockSpec(memory_space=pl.ANY)],
+        out_specs=pl.BlockSpec(memory_space=pltpu.VMEM),
+        scratch_shapes=[pltpu.SemaphoreType.DMA],
+        cost_estimate=pl.CostEstimate(flops=0, bytes_accessed=2 * x.size * x.dtype.itemsize, transcendentals=0),
+        name="fetched",
+    )(x)
+
+
+def down_kernel(groups, hidden_ref, down_ref, out_ref, held, sems):
+    ranks, units = hidden_ref.shape[:2]
+    size = CHUNK * ranks * PADDED
     copies = []
     for i in range(groups // CHUNK):
-        part = pl.ds(i * CHUNK, CHUNK)
+        part = pl.ds(i * size, size)
         copy = pltpu.make_async_copy(down_ref.at[part], held.at[part], sems.at[i])
         copy.start()
         copies.append(copy)
-    features = CHUNK * padded
+    features = CHUNK * PADDED
     for i, copy in enumerate(copies):
         copy.wait()
+
+        def block(rank):
+            starts = [i * size + (group * ranks + rank) * PADDED for group in range(CHUNK)]
+            return jnp.concatenate([held[start : start + PADDED, :] for start in starts], axis=0)
+
         total = None
         for j in range(0, ranks, 2):
-            block = jnp.concatenate(
-                [held[i * CHUNK : (i + 1) * CHUNK, k].reshape(features, units) for k in (j, j + 1)], axis=1
-            )
+            both = jnp.concatenate([block(j), block(j + 1)], axis=1)
             hidden = hidden_ref[j : j + 2].reshape(2 * units, -1)
-            terms = jnp.dot(block, hidden, preferred_element_type=jnp.float32)
+            terms = jnp.dot(both, hidden, preferred_element_type=jnp.float32)
             total = terms if total is None else total + terms
         out_ref[:, i * features : (i + 1) * features] = total.T
 
 
 def down_projection(hidden, down):
     ranks, units, rows = hidden.shape
-    groups = down.shape[0]
+    groups = down.shape[0] // (ranks * PADDED)
     features = groups * PADDED
     return pl.pallas_call(
-        down_kernel,
+        functools.partial(down_kernel, groups),
         out_shape=jax.ShapeDtypeStruct((rows, features), jnp.float32),
         in_specs=[pl.BlockSpec(memory_space=pltpu.VMEM), pl.BlockSpec(memory_space=pl.ANY)],
         out_specs=pl.BlockSpec(memory_space=pltpu.VMEM),
@@ -117,7 +139,7 @@
 
     split = jnp.pad(down_weight.T.reshape(ranks, each, units), ((0, 0), (0, PADDED - each), (0, 0)))
     mine = lax.all_to_all(split, "tp", 0, 0)
-    down = lax.all_gather(mine, "dp", axis=0, tiled=False)
+    down = lax.all_gather(mine.reshape(-1, units), "dp", axis=0, tiled=True)
 
     normed, mine = lax.optimization_barrier((normalize(resid, norm_gain), mine))
     gathered = to_all(normed, ranks).reshape(ranks * own_rows, width)
@@ -128,7 +150,7 @@
     live = lax.broadcasted_iota(jnp.int32, (own_rows, LANES), 0) < row_count[0]
     own = jnp.concatenate([residual_rows.astype(jnp.float32), live.astype(jnp.float32)], axis=1)
     hidden, own = lax.optimization_barrier((hidden.T, own))
-    hidden = to_all(hidden, ranks)
+    hidden = fetched(to_all(hidden, ranks))
 
     total = down_projection(hidden, down)
     parts = lax.all_to_all(total.reshape(ranks, own_rows, -1), "tp", 0, 0)

time: 139 us -> 139 us (level)
  waiting for transfers between devices: 30.3 us -> 26.8 us
  local copies, waits for them, and re-layouts: 4.12 us -> 5.86 us
  Pallas kernels: 9.4 us -> 11 us
    all_gather x1, waiting for transfers between devices: 8.87 us -> 5.35 us  [shards(): down = lax.all_gather(mine.reshape(-1, units), 'dp', axis=0, tiled=True)]
    unnamed x8 -> x10, local copies, waits for them, and re-layouts: 0.92 us -> 2.66 us
    pallas_call x1 -> x2, Pallas kernels: 7.13 us -> 8.72 us  [the longest x1 5.39 us: down_projection(): pl.pallas_call(functools.partial(down_kernel, groups), out_shape=jax.Shap...]
  transfers between devices with their start and end apart: 2 -> 2, of which waited for: 2 -> 2; matrix products, arithmetic and copies ran while one was open for 9% -> 9% of each run, Pallas kernels for 0% -> 2%
where the time goes in v10:
time: 139 us
  blocking collectives  67.1 us (48%)
  waiting for transfers between devices  26.8 us (19%)
  between operations  14.1 us (10%)
  Pallas kernels  11 us (8%)
  matrix products  7.28 us (5%)
  local copies, waits for them, and re-layouts  5.86 us (4%)
  starting transfers between devices  3.71 us (3%)
  other arithmetic  2.83 us (2%)
    all_to_all x1, blocking collectives, to_all(): lax.all_to_all(jnp.broadcast_to(x[None], (ranks, *x.shape)), 'tp', 0, 0)  36.9 us
    all_to_all x1, waiting for transfers between devices, to_all(): lax.all_to_all(jnp.broadcast_to(x[None], (ranks, *x.shape)), 'tp', 0, 0)  21.4 us
    all_to_all x1, blocking collectives, shards(): mine = lax.all_to_all(split, 'tp', 0, 0)  15.4 us
    all_to_all x1, blocking collectives, shards(): parts = lax.all_to_all(total.reshape(ranks, own_rows, -1), 'tp', 0, 0)  14.8 us
    dot_general x1, matrix products, shards(): gate = jnp.dot(gathered, gate_weight, preferred_element_type=jnp.float32)  5.58 us
    pallas_call x1, Pallas kernels, down_projection(): pl.pallas_call(functools.partial(down_kernel, groups), out_shape=jax.Shap...  5.39 us
    all_gather x1, waiting for transfers between devices, shards(): down = lax.all_gather(mine.reshape(-1, units), 'dp', axis=0, tiled=True)  5.35 us
    all_to_all x1, starting transfers between devices, to_all(): lax.all_to_all(jnp.broadcast_to(x[None], (ranks, *x.shape)), 'tp', 0, 0)  3.71 us
  transfers between devices with their start and end apart: 2, of which 2 were waited for; matrix products, arithmetic and copies ran while one was open for 9% of the time, Pallas kernels for 2%

profile of v10, /device:TPU:1, one launch (start us, length us, event | category | flops | bytes accessed | tf_op | source)
XLA Modules:
  0.0 138.7 jit_solution(11686729110777265302)
XLA Ops:
  6.5 1.0 reshape.23
  7.6 15.4 %all_to_all.20 = bf16[16,16,640]{2,1,0:T(8,128)(2,1)} all-to-all(bf16[16,16,640]{2,1,0:T(8,128)(2,1)S(1)} %pad.4), channel_id=1, replica_groups=mesh['dp'=32,'tp'=16] {'tp'}, dimensions={0} | all-to-all | bytes 655360 | tf_op jit(solution)/shard_map/all_to_all | solution.py:141
  23.0 0.0 all-gather.2.cloned.1.call-update
  23.0 1.1 fusion.2
  24.1 1.0 fusion.4
  25.1 1.4 %broadcast_in_dim.4 = bf16[16,8,7168]{2,1,0:T(8,128)(2,1)} broadcast(bf16[8,7168]{1,0:T(8,128)(2,1)S(1)} %fusion.4), dimensions={1,2} | broadcast | bytes 1949696 | tf_op jit(solution)/shard_map/broadcast_in_dim | solution.py:130
  26.5 3.7 %all-to-all-start.1 = ((bf16[16,8,7168]{2,1,0:T(8,128)(2,1)}), bf16[16,8,7168]{2,1,0:T(8,128)(2,1)S(1)}, u32[]{:S(2)}, u32[]{:S(2)}) async-start(bf16[16,8,7168]{2,1,0:T(8,128)(2,1)} %broadcast_in_dim.4), calls=%async_computation.1 | async-start | bytes 3670016 | tf_op jit(solution)/shard_map/all_to_all | solution.py:130
  30.9 21.4 %all-to-all-done.1 = bf16[16,8,7168]{2,1,0:T(8,128)(2,1)S(1)} async-done(((bf16[16,8,7168]{2,1,0:T(8,128)(2,1)}), bf16[16,8,7168]{2,1,0:T(8,128)(2,1)S(1)}, u32[]{:S(2)}, u32[]{:S(2)}) %all-to-all-start.1) | async-done | bytes 1835040 | tf_op jit(solution)/shard_map/all_to_all | solution.py:130
  52.3 0.0 slice-start.1
  52.3 5.6 %convolution_bitcast_fusion.1 = f32[640,128]{0,1:T(8,128)S(1)} fusion(bf16[128,7168]{1,0:T(8,128)(2,1)S(1)} %bitcast.19, bf16[7168,640]{1,0:T(8,128)(2,1)} %param.8), kind=kOutput, calls=%fused_computation.1 | convolution fusion | flops 1174405120 | bytes 11337728 | tf_op jit(solution)/shard_map/dot_general | solution.py:147
  57.9 0.8 slice-done.1
  58.7 0.1 slice-done.2
  58.8 1.7 %fusion.1 = bf16[640,128]{0,1:T(8,128)(2,1)S(1)} fusion(bf16[128,7168]{1,0:T(8,128)(2,1)S(1)} %bitcast.20, bf16[7168,640]{1,0:T(8,128)(2,1)S(1)} %bitcast.22, f32[640,128]{0,1:T(8,128)S(1)} %convolution_bitcast_fusion.1), kind=kOutput, calls=%fused_computation.3 | convolution fusion | flops 1174896640 | bytes 11501568 | tf_op jit(solution)/shard_map/dot_general | solution.py:148
  60.5 0.1 iota.7
  60.6 0.7 pad_maximum_fusion.own_ref
  61.3 0.2 copy.8
  61.5 0.5 broadcast_in_dim.5
  62.0 36.9 %all_to_all.21.x_ref = bf16[16,640,128]{2,1,0:T(8,128)(2,1)} all-to-all(bf16[16,640,128]{2,1,0:T(8,128)(2,1)S(1)} %broadcast_in_dim.5), channel_id=1, replica_groups=mesh['dp'=32,'tp'=16] {'tp'}, dimensions={0} | all-to-all | bytes 5242880 | tf_op jit(solution)/shard_map/all_to_all | solution.py:130
  99.0 3.3 %fetched.1.hidden_ref = bf16[16,640,128]{2,1,0:T(8,128)(2,1)} custom-call(bf16[16,640,128]{2,1,0:T(8,128)(2,1)} %all_to_all.21.x_ref), custom_call_target="tpu_custom_call" | custom-call | bytes 5242880 | tf_op jit(solution)/shard_map/fetched/pallas_call | solution.py:28
  102.3 5.4 %all-gather.2.cloned.1.call-done.down_ref = bf16[8192,640]{1,0:T(8,128)(2,1)} async-done(((bf16[256,640]{1,0:T(8,128)(2,1)}), bf16[8192,640]{1,0:T(8,128)(2,1)}) %all-gather.2.cloned.1.call-update) | async-done | bytes 10485776 | tf_op jit(solution)/shard_map/all_gather | solution.py:142
  107.6 1.7 %copy-done = bf16[16,640,128]{2,1,0:T(8,128)(2,1)S(1)} copy-done((bf16[16,640,128]{2,1,0:T(8,128)(2,1)S(1)}, bf16[16,640,128]{2,1,0:T(8,128)(2,1)}, u32[]{:S(2)}) %copy-start) | copy-done | bytes 2621464
  109.4 5.4 %down_projection.1 = f32[128,512]{1,0:T(8,128)S(1)} custom-call(bf16[16,640,128]{2,1,0:T(8,128)(2,1)S(1)} %copy-done, bf16[8192,640]{1,0:T(8,128)(2,1)} %all-gather.2.cloned.1.call-done.down_ref), custom_call_target="tpu_custom_call" | custom-call | flops 1342177280 | bytes 13107200 | tf_op jit(solution)/shard_map/down_projection/pallas_call | solution.py:69
  114.8 14.8 %all_to_all.22.parts_ref = f32[16,8,512]{2,1,0:T(8,128)} all-to-all(f32[16,8,512]{2,1,0:T(8,128)S(1)} %bitcast.18), channel_id=1, replica_groups=mesh['dp'=32,'tp'=16] {'tp'}, dimensions={0} | all-to-all | bytes 524288 | tf_op jit(solution)/shard_map/all_to_all | solution.py:156
  129.6 2.3 %finish.1 = bf16[8,7168]{1,0:T(8,128)(2,1)} custom-call(f32[16,8,512]{2,1,0:T(8,128)} %all_to_all.22.parts_ref, f32[8,7296]{1,0:T(8,128)} %pad_maximum_fusion.own_ref), custom_call_target="tpu_custom_call" | custom-call | tf_op jit(solution)/shard_map/finish/pallas_call | solution.py:120
  (12 shorter events, 0.1 us)
Async XLA Ops:
  6.5 101.1 %all-gather.2.cloned.1.call-start = ((), (), s32[]{:S(2)}) async-start(), calls=%async_computation.4 | async-start | bytes 10813440 | tf_op jit(solution)/shard_map/all_gather | solution.py:142
  25.1 27.2 %copy-start.1 = (bf16[8,7168]{1,0:T(8,128)(2,1)S(1)}, bf16[8,7168]{1,0:T(8,128)(2,1)}, u32[]{:S(2)}) copy-start(bf16[8,7168]{1,0:T(8,128)(2,1)} %param.6) | copy-start | bytes 344068
  26.5 25.8 %all-to-all-start.1 = ((bf16[16,8,7168]{2,1,0:T(8,128)(2,1)}), bf16[16,8,7168]{2,1,0:T(8,128)(2,1)S(1)}, u32[]{:S(2)}, u32[]{:S(2)}) async-start(bf16[16,8,7168]{2,1,0:T(8,128)(2,1)} %broadcast_in_dim.4), calls=%async_computation.1 | async-start | bytes 3670016 | tf_op jit(solution)/shard_map/all_to_all | solution.py:130
  52.3 5.6 %slice-start = ((s8[9175040]{0:T(1024)(128)(4,1)}), s8[4194304]{0:T(1024)(128)(4,1)S(1)}, s32[]{:S(2)}) async-start(s8[9175040]{0:T(1024)(128)(4,1)} %bitcast.21), calls=%async_computation.5 | async-start | bytes 8388608
  52.3 6.4 %slice-start.1 = ((s8[9175040]{0:T(1024)(128)(4,1)}), s8[4194304]{0:T(1024)(128)(4,1)S(1)}, s32[]{:S(2)}) async-start(s8[9175040]{0:T(1024)(128)(4,1)} %bitcast.21), calls=%async_computation.6 | async-start | bytes 8388608
  52.3 6.5 %slice-start.2 = ((s8[9175040]{0:T(1024)(128)(4,1)}), s8[786432]{0:T(1024)(128)(4,1)S(1)}, s32[]{:S(2)}) async-start(s8[9175040]{0:T(1024)(128)(4,1)} %bitcast.21), calls=%async_computation.7 | async-start | bytes 1572864
  107.6 1.7 %copy-start = (bf16[16,640,128]{2,1,0:T(8,128)(2,1)S(1)}, bf16[16,640,128]{2,1,0:T(8,128)(2,1)}, u32[]{:S(2)}) copy-start(bf16[16,640,128]{2,1,0:T(8,128)(2,1)} %fetched.1.hidden_ref) | copy-start | bytes 7864324
Sparse Core Ops, SparseCore 0:
  23.2 84.4 all-gather.1

commit v11 on v10

--- a/solution.py
+++ b/solution.py
@@ -31,6 +31,7 @@
         in_specs=[pl.BlockSpec(memory_space=pl.ANY)],
         out_specs=pl.BlockSpec(memory_space=pltpu.VMEM),
         scratch_shapes=[pltpu.SemaphoreType.DMA],
+        compiler_params=pltpu.CompilerParams(vmem_limit_bytes=8 * 1024 * 1024),
         cost_estimate=pl.CostEstimate(flops=0, bytes_accessed=2 * x.size * x.dtype.itemsize, transcendentals=0),
         name="fetched",
     )(x)

time: 139 us -> 137 us (0.986)
  Pallas kernels: 11 us -> 7.84 us
  waiting for transfers between devices: 26.8 us -> 29.1 us
  local copies, waits for them, and re-layouts: 5.86 us -> 4.12 us
    pallas_call x1, Pallas kernels: 3.33 us -> 0.19 us  [fetched(): pl.pallas_call(fetch_kernel, out_shape=jax.ShapeDtypeStruct(x.shape, x.dt...]
    all_gather x1, waiting for transfers between devices: 5.35 us -> 7.72 us  [shards(): down = lax.all_gather(mine.reshape(-1, units), 'dp', axis=0, tiled=True)]
    unnamed x10 -> x8, local copies, waits for them, and re-layouts: 2.66 us -> 0.92 us
  transfers between devices with their start and end apart: 2 -> 2, of which waited for: 2 -> 2; matrix products, arithmetic and copies ran while one was open for 9% -> 9% of each run, Pallas kernels for 2% -> 0%
where the time goes in v11:
time: 137 us
  blocking collectives  67.8 us (49%)
  waiting for transfers between devices  29.1 us (21%)
  between operations  14.1 us (10%)
  Pallas kernels  7.84 us (6%)
  matrix products  7.27 us (5%)
  local copies, waits for them, and re-layouts  4.12 us (3%)
  starting transfers between devices  3.71 us (3%)
  other arithmetic  2.83 us (2%)
    all_to_all x1, blocking collectives, to_all(): lax.all_to_all(jnp.broadcast_to(x[None], (ranks, *x.shape)), 'tp', 0, 0)  37.8 us
    all_to_all x1, waiting for transfers between devices, to_all(): lax.all_to_all(jnp.broadcast_to(x[None], (ranks, *x.shape)), 'tp', 0, 0)  21.4 us
    all_to_all x1, blocking collectives, shards(): mine = lax.all_to_all(split, 'tp', 0, 0)  15.4 us
    all_to_all x1, blocking collectives, shards(): parts = lax.all_to_all(total.reshape(ranks, own_rows, -1), 'tp', 0, 0)  14.6 us
    all_gather x1, waiting for transfers between devices, shards(): down = lax.all_gather(mine.reshape(-1, units), 'dp', axis=0, tiled=True)  7.72 us
    dot_general x1, matrix products, shards(): gate = jnp.dot(gathered, gate_weight, preferred_element_type=jnp.float32)  5.58 us
    pallas_call x1, Pallas kernels, down_projection(): pl.pallas_call(functools.partial(down_kernel, groups), out_shape=jax.Shap...  5.39 us
    all_to_all x1, starting transfers between devices, to_all(): lax.all_to_all(jnp.broadcast_to(x[None], (ranks, *x.shape)), 'tp', 0, 0)  3.71 us
  transfers between devices with their start and end apart: 2, of which 2 were waited for; matrix products, arithmetic and copies ran while one was open for 9% of the time, Pallas kernels for 0%

profile of v11, /device:TPU:1, one launch (start us, length us, event | category | flops | bytes accessed | tf_op | source)
XLA Modules:
  0.0 136.9 jit_solution(4133198830733292047)
XLA Ops:
  6.5 1.0 reshape.23
  7.6 15.4 %all_to_all.20 = bf16[16,16,640]{2,1,0:T(8,128)(2,1)} all-to-all(bf16[16,16,640]{2,1,0:T(8,128)(2,1)S(1)} %pad.4), channel_id=1, replica_groups=mesh['dp'=32,'tp'=16] {'tp'}, dimensions={0} | all-to-all | bytes 655360 | tf_op jit(solution)/shard_map/all_to_all | solution.py:142
  23.0 0.0 all-gather.2.cloned.1.call-update
  23.0 1.1 fusion.2
  24.1 1.0 fusion.4
  25.1 0.0 copy-start
  25.1 1.4 %broadcast_in_dim.4 = bf16[16,8,7168]{2,1,0:T(8,128)(2,1)} broadcast(bf16[8,7168]{1,0:T(8,128)(2,1)S(1)} %fusion.4), dimensions={1,2} | broadcast | bytes 1949696 | tf_op jit(solution)/shard_map/broadcast_in_dim | solution.py:131
  26.5 3.7 %all-to-all-start.1 = ((bf16[16,8,7168]{2,1,0:T(8,128)(2,1)}), bf16[16,8,7168]{2,1,0:T(8,128)(2,1)S(1)}, u32[]{:S(2)}, u32[]{:S(2)}) async-start(bf16[16,8,7168]{2,1,0:T(8,128)(2,1)} %broadcast_in_dim.4), calls=%async_computation.1 | async-start | bytes 3670016 | tf_op jit(solution)/shard_map/all_to_all | solution.py:131
  30.9 21.4 %all-to-all-done.1 = bf16[16,8,7168]{2,1,0:T(8,128)(2,1)S(1)} async-done(((bf16[16,8,7168]{2,1,0:T(8,128)(2,1)}), bf16[16,8,7168]{2,1,0:T(8,128)(2,1)S(1)}, u32[]{:S(2)}, u32[]{:S(2)}) %all-to-all-start.1) | async-done | bytes 1835040 | tf_op jit(solution)/shard_map/all_to_all | solution.py:131
  52.3 0.0 slice-start.1
  52.3 5.6 %convolution_bitcast_fusion.1 = f32[640,128]{0,1:T(8,128)S(1)} fusion(bf16[128,7168]{1,0:T(8,128)(2,1)S(1)} %bitcast.19, bf16[7168,640]{1,0:T(8,128)(2,1)} %param.8), kind=kOutput, calls=%fused_computation.1 | convolution fusion | flops 1174405120 | bytes 11337728 | tf_op jit(solution)/shard_map/dot_general | solution.py:148
  57.9 0.8 slice-done.1
  58.7 0.1 slice-done.2
  58.8 1.7 %fusion.1 = bf16[640,128]{0,1:T(8,128)(2,1)S(1)} fusion(bf16[128,7168]{1,0:T(8,128)(2,1)S(1)} %bitcast.20, bf16[7168,640]{1,0:T(8,128)(2,1)S(1)} %bitcast.22, f32[640,128]{0,1:T(8,128)S(1)} %convolution_bitcast_fusion.1), kind=kOutput, calls=%fused_computation.3 | convolution fusion | flops 1174896640 | bytes 11501568 | tf_op jit(solution)/shard_map/dot_general | solution.py:149
  60.5 0.1 iota.7
  60.6 0.7 pad_maximum_fusion.own_ref
  61.3 0.2 copy.8
  61.5 0.5 broadcast_in_dim.5
  62.0 37.8 %all_to_all.21.x_ref = bf16[16,640,128]{2,1,0:T(8,128)(2,1)S(1)} all-to-all(bf16[16,640,128]{2,1,0:T(8,128)(2,1)S(1)} %broadcast_in_dim.5), channel_id=1, replica_groups=mesh['dp'=32,'tp'=16] {'tp'}, dimensions={0} | all-to-all | bytes 5242880 | tf_op jit(solution)/shard_map/all_to_all | solution.py:131
  99.8 0.2 fetched.1.hidden_ref
  100.0 7.7 %all-gather.2.cloned.1.call-done.down_ref = bf16[8192,640]{1,0:T(8,128)(2,1)} async-done(((bf16[256,640]{1,0:T(8,128)(2,1)}), bf16[8192,640]{1,0:T(8,128)(2,1)}) %all-gather.2.cloned.1.call-update) | async-done | bytes 10485776 | tf_op jit(solution)/shard_map/all_gather | solution.py:143
  107.8 5.4 %down_projection.1 = f32[128,512]{1,0:T(8,128)S(1)} custom-call(bf16[16,640,128]{2,1,0:T(8,128)(2,1)S(1)} %fetched.1.hidden_ref, bf16[8192,640]{1,0:T(8,128)(2,1)} %all-gather.2.cloned.1.call-done.down_ref), custom_call_target="tpu_custom_call" | custom-call | flops 1342177280 | bytes 13107200 | tf_op jit(solution)/shard_map/down_projection/pallas_call | solution.py:70
  113.2 14.6 %all_to_all.22.parts_ref = f32[16,8,512]{2,1,0:T(8,128)} all-to-all(f32[16,8,512]{2,1,0:T(8,128)S(1)} %bitcast.18), channel_id=1, replica_groups=mesh['dp'=32,'tp'=16] {'tp'}, dimensions={0} | all-to-all | bytes 524288 | tf_op jit(solution)/shard_map/all_to_all | solution.py:157
  127.8 2.3 %finish.1 = bf16[8,7168]{1,0:T(8,128)(2,1)} custom-call(f32[16,8,512]{2,1,0:T(8,128)} %all_to_all.22.parts_ref, f32[8,7296]{1,0:T(8,128)} %pad_maximum_fusion.own_ref), custom_call_target="tpu_custom_call" | custom-call | tf_op jit(solution)/shard_map/finish/pallas_call | solution.py:121
  (10 shorter events, 0.1 us)
Async XLA Ops:
  6.5 101.2 %all-gather.2.cloned.1.call-start = ((), (), s32[]{:S(2)}) async-start(), calls=%async_computation.4 | async-start | bytes 10813440 | tf_op jit(solution)/shard_map/all_gather | solution.py:143
  25.1 27.2 %copy-start = (bf16[8,7168]{1,0:T(8,128)(2,1)S(1)}, bf16[8,7168]{1,0:T(8,128)(2,1)}, u32[]{:S(2)}) copy-start(bf16[8,7168]{1,0:T(8,128)(2,1)} %param.6) | copy-start | bytes 344068
  26.5 25.8 %all-to-all-start.1 = ((bf16[16,8,7168]{2,1,0:T(8,128)(2,1)}), bf16[16,8,7168]{2,1,0:T(8,128)(2,1)S(1)}, u32[]{:S(2)}, u32[]{:S(2)}) async-start(bf16[16,8,7168]{2,1,0:T(8,128)(2,1)} %broadcast_in_dim.4), calls=%async_computation.1 | async-start | bytes 3670016 | tf_op jit(solution)/shard_map/all_to_all | solution.py:131
  52.3 5.6 %slice-start = ((s8[9175040]{0:T(1024)(128)(4,1)}), s8[4194304]{0:T(1024)(128)(4,1)S(1)}, s32[]{:S(2)}) async-start(s8[9175040]{0:T(1024)(128)(4,1)} %bitcast.21), calls=%async_computation.5 | async-start | bytes 8388608
  52.3 6.4 %slice-start.1 = ((s8[9175040]{0:T(1024)(128)(4,1)}), s8[4194304]{0:T(1024)(128)(4,1)S(1)}, s32[]{:S(2)}) async-start(s8[9175040]{0:T(1024)(128)(4,1)} %bitcast.21), calls=%async_computation.6 | async-start | bytes 8388608
  52.3 6.5 %slice-start.2 = ((s8[9175040]{0:T(1024)(128)(4,1)}), s8[786432]{0:T(1024)(128)(4,1)S(1)}, s32[]{:S(2)}) async-start(s8[9175040]{0:T(1024)(128)(4,1)} %bitcast.21), calls=%async_computation.7 | async-start | bytes 1572864
Sparse Core Ops, SparseCore 0:
  23.2 84.5 all-gather.1
